TPU v7x, 512 devices: a whole 4x8x8 slice. The times are simulated.
512 devices in a mesh: replica: 32 (over z, y_hi, core), fsdp: 16 (over x, y_lo).
Axes of the slice: x: 4, y: 8 (y_hi: 2, y_lo: 4; y = y_hi * 4 + y_lo), z: 8, core: 2. Of those that a mesh axis runs over, the one named last changes fastest.
Arguments:
- inputs: bfloat16 [32, 4096, 4096], P('replica', 'fsdp'), may hold values from -6 to 6
- targets: bfloat16 [32, 4096, 1024], P('replica', 'fsdp'), may hold values from -6 to 6
- local_weight: bfloat16 [32, 4096, 1024], P('replica', 'fsdp'), may hold values from -0.09375 to 0.09375
- outer_params: float32 [4, 4096, 1024], P(None, ('fsdp', 'replica')), may hold values from -0.09375 to 0.09375
- outer_moment: float32 [4, 4096, 1024], P(None, ('fsdp', 'replica')), may hold values from -0.06 to 0.06
- fragment: int32 [1], replicated, may hold values from 0 to 16383
Outputs:
- merged_weight: float32 [32, 4096, 1024], P('replica', 'fsdp')
- new_params: float32 [4, 4096, 1024], P(None, ('fsdp', 'replica'))
- new_moment: float32 [4, 4096, 1024], P(None, ('fsdp', 'replica'))
All inputs are finite; a program needn't handle non-finite values.
Results may differ from a plain program's by a relative error of at most 0.0027.
Values may be sent and summed in bfloat16 or wider, within the bound.
No kernel may reach another device: no remote copies, remote signals or barrier semaphores. Data moves between devices by JAX's collectives and lax.ppermute only.
A program may use at most 64 MiB of HBM per device.

v0:
```python
import jax
import jax.numpy as jnp
from jax import lax
from jax.sharding import PartitionSpec as P

inner_rate = 1.0
outer_rate = 0.7
moment_keep = 0.9
merge_share = 0.5


def on_device(inputs, targets, local_weight, outer_params, outer_moment, fragment):
    which = jnp.remainder(fragment[0], jnp.int32(outer_params.shape[0]))
    own_rows = local_weight[0]
    tokens = inputs[0]
    wanted = targets[0]
    g_piece = lax.dynamic_index_in_dim(outer_params, which, 0, keepdims=False)
    m_piece = lax.dynamic_index_in_dim(outer_moment, which, 0, keepdims=False)
    replicas = lax.axis_size("replica")
    g_full, m_full = (
        lax.all_gather(g_piece, "replica", axis=0, tiled=True),
        lax.all_gather(m_piece, "replica", axis=0, tiled=True),
    )
    summed = lax.psum(own_rows.astype(jnp.float32), "replica")
    outer_grad = g_full - summed / replicas
    moment_full = moment_keep * m_full + outer_grad
    global_next = g_full - outer_rate * (outer_grad + moment_keep * moment_full)
    row_count = g_piece.shape[0]
    offset = lax.axis_index("replica") * row_count
    global_keep = lax.dynamic_slice_in_dim(global_next, offset, row_count, 0)
    moment_kept = lax.dynamic_slice_in_dim(moment_full, offset, row_count, 0)
    projected = jnp.dot(
        tokens,
        lax.all_gather(own_rows, "fsdp", axis=0, tiled=True),
        preferred_element_type=jnp.float32,
    )
    residual = (projected - wanted.astype(jnp.float32)).astype(jnp.bfloat16)
    my_columns = lax.all_to_all(tokens, "fsdp", split_axis=1, concat_axis=0, tiled=True)
    gradient = lax.dot_general(
        my_columns,
        lax.all_gather(residual, "fsdp", axis=0, tiled=True),
        (((0,), (0,)), ((), ())),
        preferred_element_type=jnp.float32,
    )
    all_tokens = tokens.shape[0] * lax.axis_size("fsdp")
    stepped = own_rows.astype(jnp.float32) - inner_rate * (gradient / all_tokens)
    merged = merge_share * stepped + (1.0 - merge_share) * global_next
    new_params = lax.dynamic_update_index_in_dim(outer_params, global_keep, which, 0)
    new_moment = lax.dynamic_update_index_in_dim(outer_moment, moment_kept, which, 0)
    return (merged[None], new_params, new_moment)


def solution(mesh):
    placed = (
        P("replica", "fsdp", None),
        P("replica", "fsdp", None),
        P("replica", "fsdp", None),
        P(None, ("fsdp", "replica"), None),
        P(None, ("fsdp", "replica"), None),
        P(),
    )
    return jax.shard_map(
        on_device,
        mesh=mesh,
        in_specs=placed,
        out_specs=(
            P("replica", "fsdp", None),
            P(None, ("fsdp", "replica"), None),
            P(None, ("fsdp", "replica"), None),
        ),
        check_vma=False,
    )
```

profile of v0, /device:TPU:1, one launch (start us, length us, event | category | flops | bytes accessed | tf_op | source)
XLA Modules:
  0.0 932.3 jit_solution(17668812873268889028)
XLA Ops:
  7.2 0.0 all-gather.10.cloned.1.call-start
  7.2 0.9 copy.45
  8.1 0.9 copy.46
  9.0 0.0 all-gather.10.cloned.1.call-update
  9.0 0.0 copy-start.2
  9.1 0.0 all-gather.12.cloned.1.call-start
  9.9 0.6 copy.37
  10.6 0.0 all-gather.12.cloned.1.call-update
  10.6 0.0 all-gather.14.cloned.1.call-start
  10.7 0.6 copy.38
  11.3 0.0 all-gather.14.cloned.1.call-update
  11.3 0.0 all-reduce.2.cloned.1.call-start
  11.4 1.2 copy.27
  12.6 0.0 copy-start.1
  12.7 1.1 bitcast_convert_fusion
  13.8 0.0 all-reduce.2.cloned.1.call-update
  13.8 0.0 all-gather.8.cloned.1.call-start
  13.9 191.9 %all-gather.10.cloned.1.call-done = bf16[1,4096,1024]{2,1,0:T(8,128)(2,1)} async-done(((bf16[1,256,1024]{2,1,0:T(8,128)(2,1)}), bf16[1,4096,1024]{2,1,0:T(8,128)(2,1)}) %all-gather.10.cloned.1.call-update) | async-done | bytes 8388624 | tf_op jit(solution)/shard_map/all_gather | solution.py:34
  205.7 0.0 copy-done.2
  205.7 6.6 fusion.13
  212.3 0.0 copy-done.1
  212.3 0.0 all-gather.8.cloned.1.call-update
  212.3 2.6 copy.28
  214.9 3.9 all-to-all-start
  218.7 75.5 %all-gather.12.cloned.1.call-done = f32[1,256,1024]{2,0,1:T(1,128)} async-done(((f32[1,8,1024]{2,0,1:T(1,128)}), f32[1,256,1024]{2,0,1:T(1,128)}) %all-gather.12.cloned.1.call-update) | async-done | bytes 1048592 | tf_op jit(solution)/shard_map/all_gather | solution.py:21
  294.2 3.6 copy.31
  297.8 83.7 %all-gather.14.cloned.1.call-done = f32[1,256,1024]{2,0,1:T(1,128)} async-done(((f32[1,8,1024]{2,0,1:T(1,128)}), f32[1,256,1024]{2,0,1:T(1,128)}) %all-gather.14.cloned.1.call-update) | async-done | bytes 1048592 | tf_op jit(solution)/shard_map/all_gather | solution.py:22
  381.4 3.6 copy.33
  385.0 340.9 %all-reduce.2.cloned.1.call-done = f32[256,1024]{0,1:T(8,128)} async-done(((f32[256,1024]{0,1:T(8,128)}), f32[256,1024]{0,1:T(8,128)}) %all-reduce.2.cloned.1.call-update) | async-done | bytes 1048592 | tf_op jit(solution)/shard_map/psum | solution.py:24
  725.9 3.1 bitcast_add_fusion
  729.1 1.0 constant_dynamic-slice_fusion.1
  730.1 1.2 copy.34
  731.3 2.1 constant_dynamic-slice_fusion
  733.3 1.2 copy.35
  734.5 0.0 copy-start.3
  734.6 0.0 copy-start.4
  734.6 0.0 all-to-all-done
  734.6 0.0 copy-start
  734.6 1.4 copy-done
  736.0 2.8 copy.29
  738.9 177.5 %all-gather.8.cloned.1.call-done = bf16[4096,1024]{1,0:T(8,128)(2,1)} async-done(((bf16[256,1024]{1,0:T(8,128)(2,1)}), bf16[4096,1024]{1,0:T(8,128)(2,1)}) %all-gather.8.cloned.1.call-update) | async-done | bytes 8388624 | tf_op jit(solution)/shard_map/all_gather | solution.py:41
  916.4 6.9 fusion.7
  923.2 0.0 copy-done.3
  923.2 0.0 copy-done.4
  923.2 2.5 copy.36
  (3 shorter events, 0.0 us)
Async XLA Ops:
  7.2 198.6 %all-gather.10.cloned.1.call-start = ((), (), s32[]{:S(2)}) async-start(), calls=%async_computation.3 | async-start | bytes 8912896 | tf_op jit(solution)/shard_map/all_gather | solution.py:34
  9.0 196.7 %copy-start.2 = (bf16[1,256,4096]{2,1,0:T(8,128)(2,1)S(1)}, bf16[1,256,4096]{2,1,0:T(8,128)(2,1)}, u32[]{:S(2)}) copy-start(bf16[1,256,4096]{2,1,0:T(8,128)(2,1)} %param.6) | copy-start | bytes 6291460
  9.1 285.1 %all-gather.12.cloned.1.call-start = ((), (), s32[]{:S(2)}) async-start(), calls=%async_computation.4 | async-start | bytes 1081344 | tf_op jit(solution)/shard_map/all_gather | solution.py:21
  10.6 370.8 %all-gather.14.cloned.1.call-start = ((), (), s32[]{:S(2)}) async-start(), calls=%async_computation.5 | async-start | bytes 1081344 | tf_op jit(solution)/shard_map/all_gather | solution.py:22
  11.3 714.6 %all-reduce.2.cloned.1.call-start = ((), (), s32[]{:S(2)}) async-start(), calls=%async_computation.2 | async-start | bytes 2097152 | tf_op jit(solution)/shard_map/psum | solution.py:24
  12.6 199.6 %copy-start.1 = (bf16[1,256,1024]{1,2,0:T(8,128)(2,1)}, bf16[1,256,1024]{1,2,0:T(8,128)(2,1)S(1)}, u32[]{:S(2)}) copy-start(bf16[1,256,1024]{1,2,0:T(8,128)(2,1)S(1)} %copy.27) | copy-start | bytes 1572868
  13.8 902.5 %all-gather.8.cloned.1.call-start = ((), (), s32[]{:S(2)}) async-start(), calls=%async_computation.1 | async-start | bytes 8912896 | tf_op jit(solution)/shard_map/all_gather | solution.py:41
  214.9 519.7 %all-to-all-start = ((bf16[256,16,256]{0,2,1:T(8,128)(2,1)}), bf16[256,16,256]{0,2,1:T(8,128)(2,1)S(1)}, u32[]{:S(2)}, u32[]{:S(2)}) async-start(bf16[256,16,256]{0,2,1:T(8,128)(2,1)} %bitcast.62), calls=%async_computation | async-start | bytes 4194304 | tf_op jit(solution)/shard_map/all_to_all | solution.py:38
  734.5 188.7 %copy-start.3 = (f32[4,8,1024]{2,1,0:T(8,128)}, f32[4,8,1024]{2,1,0:T(8,128)S(1)}, u32[]{:S(2)}) copy-start(f32[4,8,1024]{2,1,0:T(8,128)S(1)} %get-tuple-element.18) | copy-start | bytes 393220
  734.6 188.7 %copy-start.4 = (f32[4,8,1024]{2,1,0:T(8,128)}, f32[4,8,1024]{2,1,0:T(8,128)S(1)}, u32[]{:S(2)}) copy-start(f32[4,8,1024]{2,1,0:T(8,128)S(1)} %get-tuple-element.17) | copy-start | bytes 393220
  734.6 1.4 copy-start
Sparse Core Ops, SparseCore 0:
  10.1 195.5 all-gather.9
  209.7 84.4 all-gather.11
  298.2 83.2 all-gather.13
  384.2 341.6 all-reduce.1
  728.1 188.2 all-gather.7
where the time goes:
time: 933 us; the launch traced here: 932 us
  waiting for transfers between devices  869 us (93%)
  local copies, waits for them, and re-layouts  26.4 us (3%)
  between operations  14.7 us (2%)
  matrix products  13.4 us (1%)
    psum x1, waiting for transfers between devices, on_device(): summed = lax.psum(own_rows.astype(jnp.float32), 'replica')  341 us
    all_gather x1, waiting for transfers between devices, on_device(): lax.all_gather(own_rows, 'fsdp', axis=0, tiled=True)  192 us
    all_gather x1, waiting for transfers between devices, on_device(): lax.all_gather(residual, 'fsdp', axis=0, tiled=True)  177 us
    all_gather x1, waiting for transfers between devices, on_device(): lax.all_gather(m_piece, 'replica', axis=0, tiled=True)  83.7 us
    all_gather x1, waiting for transfers between devices, on_device(): lax.all_gather(g_piece, 'replica', axis=0, tiled=True)  75.5 us
  transfers between devices with their start and end apart: 6, of which 5 were waited for; matrix products, arithmetic and copies ran while one was open for 3% of the time, Pallas kernels for 0%

commit v1 on v0

v1 whole, which is shorter than its diff:
```python
import functools

import jax
import jax.numpy as jnp
from jax import lax
from jax.sharding import Mesh, PartitionSpec as P

inner_rate = 1.0
outer_rate = 0.7
moment_keep = 0.9
merge_share = 0.5

PARTS = (("z", 8), ("yh", 2), ("core", 2), ("x", 4), ("yl", 4))
REPLICA = ("z", "yh", "core")
FSDP = ("x", "yl")
CHUNKS = 2
WIRE = jnp.bfloat16


def exchange(blocks, axis):
    return lax.all_to_all(blocks, axis, 0, 0, tiled=True)


def gather(block, axis):
    n = lax.axis_size(axis)
    return exchange(jnp.broadcast_to(block[None], (n,) + block.shape), axis)


def outer_step(own_rows, g_piece, m_piece):
    nz, nh, nc = (lax.axis_size(a) for a in REPLICA)
    rows, width = own_rows.shape
    piece = rows // (nz * nh * nc)
    by_owner = own_rows.reshape(nz, nh, nc, piece, width).transpose(0, 2, 1, 3, 4)
    got = exchange(by_owner.reshape(nz * nc, nh, piece, width), ("z", "core"))
    part = jnp.sum(got.astype(jnp.float32), axis=0)
    half = lax.axis_index("yh")
    mine = lax.dynamic_index_in_dim(part, half, 0, keepdims=False)
    other = lax.dynamic_index_in_dim(part, 1 - half, 0, keepdims=False)
    summed = mine + lax.ppermute(other, "yh", [(0, 1), (1, 0)])
    outer_grad = g_piece - summed / (nz * nh * nc)
    moment = moment_keep * m_piece + outer_grad
    return g_piece - outer_rate * (outer_grad + moment_keep * moment), moment


def spread(global_keep, rows):
    nz, nh, nc = (lax.axis_size(a) for a in REPLICA)
    piece, width = global_keep.shape
    sent = global_keep.astype(WIRE)
    other = lax.ppermute(sent, "yh", [(0, 1), (1, 0)])
    first = lax.axis_index("yh") == 0
    pair = jnp.stack([jnp.where(first, sent, other), jnp.where(first, other, sent)])
    got = gather(pair, ("z", "core")).reshape(nz, nc, nh, piece, width)
    return got.transpose(0, 2, 1, 3, 4).reshape(rows, width).astype(jnp.float32)


def on_device(inputs, targets, local_weight, outer_params, outer_moment, fragment):
    which = jnp.remainder(fragment[0], jnp.int32(outer_params.shape[0]))
    own_rows, tokens, wanted = local_weight[0], inputs[0], targets[0]
    rows, width = own_rows.shape
    count = tokens.shape[0]
    nx, ny = lax.axis_size("x"), lax.axis_size("yl")
    part = width // CHUNKS

    block = exchange(
        tokens.reshape(count, nx, -1).transpose(1, 0, 2), "x"
    ).reshape(nx * count, -1)
    weights = [
        gather(own_rows[:, c * part : (c + 1) * part], "yl").reshape(ny * rows, part)
        for c in range(CHUNKS)
    ]

    g_piece = lax.dynamic_index_in_dim(outer_params, which, 0, keepdims=False)
    m_piece = lax.dynamic_index_in_dim(outer_moment, which, 0, keepdims=False)
    global_keep, moment_kept = outer_step(own_rows, g_piece, m_piece)
    global_next = spread(global_keep, rows)

    merged = []
    for c in range(CHUNKS):
        cols = slice(c * part, (c + 1) * part)
        shares = jnp.dot(block, weights[c], preferred_element_type=jnp.float32)
        got = exchange(shares.astype(WIRE).reshape(nx, count, part), "x")
        projected = jnp.sum(got.astype(jnp.float32), axis=0)
        residual = (projected - wanted[:, cols].astype(jnp.float32)).astype(jnp.bfloat16)
        all_residual = gather(residual, "x").reshape(nx * count, part)
        shares = lax.dot_general(
            block, all_residual, (((0,), (0,)), ((), ())), preferred_element_type=jnp.float32
        )
        got = exchange(shares.astype(WIRE).reshape(ny, rows, part), "yl")
        gradient = jnp.sum(got.astype(jnp.float32), axis=0) / (count * nx * ny)
        stepped = own_rows[:, cols].astype(jnp.float32) - inner_rate * gradient
        merged.append(merge_share * stepped + (1.0 - merge_share) * global_next[:, cols])
    merged = jnp.concatenate(merged, axis=1)
    new_params = lax.dynamic_update_index_in_dim(outer_params, global_keep, which, 0)
    new_moment = lax.dynamic_update_index_in_dim(outer_moment, moment_kept, which, 0)
    return (merged[None], new_params, new_moment)


def solution(mesh):
    names = tuple(n for n, _ in PARTS)
    fine = Mesh(mesh.devices.reshape([k for _, k in PARTS]), names)
    local = P(REPLICA, FSDP, None)
    outer = P(None, FSDP + REPLICA, None)
    return jax.shard_map(
        on_device,
        mesh=fine,
        in_specs=(local, local, local, outer, outer, P()),
        out_specs=(local, outer, outer),
        check_vma=False,
    )
```

time: 933 us -> 295 us (0.32)
  waiting for transfers between devices: 869 us -> 177 us
  starting transfers between devices: 4.06 us -> 69.9 us
  between operations: 14.7 us -> 1.58 us
    all_gather x4 -> x0, waiting for transfers between devices: 528 us -> none  [the longest x1 192 us: on_device(): lax.all_gather(own_rows, 'fsdp', axis=0, tiled=True)]
    psum x1 -> x0, waiting for transfers between devices: 341 us -> none  [on_device(): summed = lax.psum(own_rows.astype(jnp.float32), 'replica')]
    all_to_all x1 -> x11, waiting for transfers between devices: 0.01 us -> 176 us  [exchange(): return lax.all_to_all(blocks, axis, 0, 0, tiled=True)]
    all_to_all x1 -> x11, starting transfers between devices: 3.85 us -> 55.2 us  [exchange(): return lax.all_to_all(blocks, axis, 0, 0, tiled=True)]
    ppermute x0 -> x2, starting transfers between devices: none -> 14.7 us  [the longest x1 7.38 us: spread(): other = lax.ppermute(sent, 'yh', [(0, 1), (1, 0)])]
  transfers between devices with their start and end apart: 6 -> 13, of which waited for: 5 -> 12; matrix products, arithmetic and copies ran while one was open for 3% -> 10% of each run, Pallas kernels for 0% -> 0%
where the time goes in v1:
time: 295 us; the launch traced here: 293 us
  waiting for transfers between devices  177 us (60%)
  starting transfers between devices  69.9 us (24%)
  local copies, waits for them, and re-layouts  26.7 us (9%)
  matrix products  13.2 us (4%)
  other arithmetic  4.49 us (2%)
    all_to_all x11, waiting for transfers between devices, exchange(): return lax.all_to_all(blocks, axis, 0, 0, tiled=True)  176 us
    all_to_all x11, starting transfers between devices, exchange(): return lax.all_to_all(blocks, axis, 0, 0, tiled=True)  55.2 us
    unnamed x25, local copies, waits for them, and re-layouts  11.9 us
    dot_general x2, matrix products, on_device(): shares = jnp.dot(block, weights[c], preferred_element_type=jnp.float32)  7.55 us
    ppermute x1, starting transfers between devices, spread(): other = lax.ppermute(sent, 'yh', [(0, 1), (1, 0)])  7.38 us
    ppermute x1, starting transfers between devices, outer_step(): summed = mine + lax.ppermute(other, 'yh', [(0, 1), (1, 0)])  7.32 us
  transfers between devices with their start and end apart: 13, of which 12 were waited for; matrix products, arithmetic and copies ran while one was open for 10% of the time, Pallas kernels for 0%

profile of v1, /device:TPU:1, one launch (start us, length us, event | category | flops | bytes accessed | tf_op | source)
XLA Modules:
  0.0 293.3 jit_solution(6552120578987546016)
XLA Ops:
  0.6 0.9 copy.52
  1.5 1.6 copy.53
  3.1 1.9 copy.28
  5.0 11.8 %all-to-all-start.5 = ((bf16[16,2,8,1024]{3,2,1,0:T(8,128)(2,1)}), bf16[16,2,8,1024]{3,2,1,0:T(8,128)(2,1)S(1)}, u32[]{:S(2)}, u32[]{:S(2)}) async-start(bf16[16,2,8,1024]{3,2,1,0:T(8,128)(2,1)} %bitcast.13), calls=%async_computation.5 | async-start | bytes 1048576 | tf_op jit(solution)/shard_map/all_to_all | solution.py:21
  16.8 3.3 %copy.22 = bf16[1,256,4096]{1,2,0:T(8,128)(2,1)S(1)} copy(bf16[1,256,4096]{2,1,0:T(8,128)(2,1)} %param.6) | data formatting | bytes 4194304 | tf_op args[0]
  20.1 2.5 copy.23
  22.6 11.5 %all-to-all-done.5 = bf16[16,2,8,1024]{3,2,1,0:T(8,128)(2,1)S(1)} async-done(((bf16[16,2,8,1024]{3,2,1,0:T(8,128)(2,1)}), bf16[16,2,8,1024]{3,2,1,0:T(8,128)(2,1)S(1)}, u32[]{:S(2)}, u32[]{:S(2)}) %all-to-all-start.5) | async-done | bytes 524320 | tf_op jit(solution)/shard_map/all_to_all | solution.py:21
  34.1 0.8 copy-done.3
  34.9 4.0 %all-to-all-start = ((bf16[4,256,1024]{2,1,0:T(8,128)(2,1)}), bf16[4,256,1024]{2,1,0:T(8,128)(2,1)S(1)}, u32[]{:S(2)}, u32[]{:S(2)}) async-start(bf16[4,256,1024]{2,1,0:T(8,128)(2,1)} %bitcast.2), calls=%async_computation | async-start | bytes 4194304 | tf_op jit(solution)/shard_map/all_to_all | solution.py:21
  38.9 0.2 copy.21
  39.2 0.1 copy.31
  39.3 25.7 %all-to-all-done = bf16[4,256,1024]{2,1,0:T(8,128)(2,1)S(1)} async-done(((bf16[4,256,1024]{2,1,0:T(8,128)(2,1)}), bf16[4,256,1024]{2,1,0:T(8,128)(2,1)S(1)}, u32[]{:S(2)}, u32[]{:S(2)}) %all-to-all-start) | async-done | bytes 2097184 | tf_op jit(solution)/shard_map/all_to_all | solution.py:21
  65.1 1.1 broadcast_in_dim.22
  66.2 4.6 %all-to-all-start.7 = ((bf16[4,256,512]{2,1,0:T(8,128)(2,1)}), bf16[4,256,512]{2,1,0:T(8,128)(2,1)}, u32[]{:S(2)}, u32[]{:S(2)}) async-start(bf16[4,256,512]{2,1,0:T(8,128)(2,1)} %broadcast_in_dim.22), calls=%async_computation.7 | async-start | bytes 2097152 | tf_op jit(solution)/shard_map/all_to_all | solution.py:21
  70.8 0.1 copy.24
  70.9 25.2 %all-to-all-done.7 = bf16[4,256,512]{2,1,0:T(8,128)(2,1)} async-done(((bf16[4,256,512]{2,1,0:T(8,128)(2,1)}), bf16[4,256,512]{2,1,0:T(8,128)(2,1)}, u32[]{:S(2)}, u32[]{:S(2)}) %all-to-all-start.7) | async-done | bytes 1048608 | tf_op jit(solution)/shard_map/all_to_all | solution.py:21
  96.2 1.1 broadcast_in_dim.18
  97.2 4.2 %all-to-all-start.1 = ((bf16[4,256,512]{2,1,0:T(8,128)(2,1)}), bf16[4,256,512]{2,1,0:T(8,128)(2,1)}, u32[]{:S(2)}, u32[]{:S(2)}) async-start(bf16[4,256,512]{2,1,0:T(8,128)(2,1)} %broadcast_in_dim.18), calls=%async_computation.1 | async-start | bytes 2097152 | tf_op jit(solution)/shard_map/all_to_all | solution.py:21
  101.5 3.5 %convolution_convert_fusion = bf16[1024,512]{1,0:T(8,128)(2,1)} fusion(bf16[1024,1024]{1,0:T(8,128)(2,1)S(1)} %bitcast.85, bf16[1024,512]{1,0:T(8,128)(2,1)} %bitcast.22), kind=kOutput, calls=%fused_computation.6 | convolution fusion | flops 1074266112 | bytes 4194304 | tf_op jit(solution)/shard_map/dot_general | solution.py:80
  105.0 21.8 %all-to-all-done.1 = bf16[4,256,512]{2,1,0:T(8,128)(2,1)} async-done(((bf16[4,256,512]{2,1,0:T(8,128)(2,1)}), bf16[4,256,512]{2,1,0:T(8,128)(2,1)}, u32[]{:S(2)}, u32[]{:S(2)}) %all-to-all-start.1) | async-done | bytes 1048608 | tf_op jit(solution)/shard_map/all_to_all | solution.py:21
  126.8 3.5 %all-to-all-start.8 = ((bf16[4,256,512]{2,1,0:T(8,128)(2,1)}), bf16[4,256,512]{2,1,0:T(8,128)(2,1)S(1)}, u32[]{:S(2)}, u32[]{:S(2)}) async-start(bf16[4,256,512]{2,1,0:T(8,128)(2,1)} %bitcast.89), calls=%async_computation.8 | async-start | bytes 2097152 | tf_op jit(solution)/shard_map/all_to_all | solution.py:21
  130.3 4.1 %convolution_convert_fusion.1 = bf16[1024,512]{1,0:T(8,128)(2,1)} fusion(bf16[1024,1024]{1,0:T(8,128)(2,1)} %bitcast.86, bf16[1024,512]{1,0:T(8,128)(2,1)} %bitcast.4), kind=kOutput, calls=%fused_computation.7 | convolution fusion | flops 1074266112 | bytes 4194304 | tf_op jit(solution)/shard_map/dot_general | solution.py:80
  134.4 9.6 %all-to-all-done.8 = bf16[4,256,512]{2,1,0:T(8,128)(2,1)S(1)} async-done(((bf16[4,256,512]{2,1,0:T(8,128)(2,1)}), bf16[4,256,512]{2,1,0:T(8,128)(2,1)S(1)}, u32[]{:S(2)}, u32[]{:S(2)}) %all-to-all-start.8) | async-done | bytes 1048608 | tf_op jit(solution)/shard_map/all_to_all | solution.py:21
  143.9 3.5 %all-to-all-start.2 = ((bf16[4,256,512]{2,1,0:T(8,128)(2,1)}), bf16[4,256,512]{2,1,0:T(8,128)(2,1)S(1)}, u32[]{:S(2)}, u32[]{:S(2)}) async-start(bf16[4,256,512]{2,1,0:T(8,128)(2,1)} %bitcast.88), calls=%async_computation.2 | async-start | bytes 2097152 | tf_op jit(solution)/shard_map/all_to_all | solution.py:21
  147.5 0.1 convert_reduce_fusion.4
  147.6 7.3 %collective-permute-start = (f32[8,1024]{1,0:T(8,128)S(1)}, f32[8,1024]{1,0:T(8,128)S(1)}, u32[]{:S(2)}, u32[]{:S(2)}) collective-permute-start(f32[8,1024]{1,0:T(8,128)S(1)} %dynamic-slice_bitcast_fusion), channel_id=1, source_target_pairs={{0,32},{32,0},{1,33},{33,1},{2,34},{34,2},{3,35},{35,3},{4,36},{36... | collective-permute-start | bytes 98312 | tf_op jit(solution)/shard_map/ppermute | solution.py:39
  155.6 0.7 collective-permute-done
  156.3 1.4 fusion.2
  157.7 7.4 %collective-permute-start.1 = (bf16[8,1024]{1,0:T(8,128)(2,1)S(1)}, bf16[8,1024]{1,0:T(8,128)(2,1)S(1)}, u32[]{:S(2)}, u32[]{:S(2)}) collective-permute-start(bf16[8,1024]{1,0:T(8,128)(2,1)S(1)} %get-tuple-element.6), channel_id=1, source_target_pairs={{0,32},{32,0},{1,33},{33,1},{2,34},{34,2},{3,35},{35,3},{4,36},{36... | collective-permute-start | bytes 49160 | tf_op jit(solution)/shard_map/ppermute | solution.py:49
  165.1 1.1 collective-permute-done.1
  166.2 0.9 broadcast_in_dim.20
  167.1 7.8 %all-to-all-start.6 = ((bf16[16,2,8,1024]{3,2,1,0:T(8,128)(2,1)}), bf16[16,2,8,1024]{3,2,1,0:T(8,128)(2,1)S(1)}, u32[]{:S(2)}, u32[]{:S(2)}) async-start(bf16[16,2,8,1024]{3,2,1,0:T(8,128)(2,1)} %broadcast_in_dim.20), calls=%async_computation.6 | async-start | bytes 1048576 | tf_op jit(solution)/shard_map/all_to_all | solution.py:21
  174.8 0.1 convert_reduce_fusion.1
  175.0 0.1 convert_reduce_fusion.3
  175.1 0.7 copy-done.5
  175.9 0.9 subtract_convert_fusion.1
  176.7 0.1 copy.32
  176.9 15.3 %all-to-all-done.6 = bf16[16,2,8,1024]{3,2,1,0:T(8,128)(2,1)S(1)} async-done(((bf16[16,2,8,1024]{3,2,1,0:T(8,128)(2,1)}), bf16[16,2,8,1024]{3,2,1,0:T(8,128)(2,1)S(1)}, u32[]{:S(2)}, u32[]{:S(2)}) %all-to-all-start.6) | async-done | bytes 524320 | tf_op jit(solution)/shard_map/all_to_all | solution.py:21
  192.2 1.0 broadcast_in_dim.44
  193.2 4.5 %all-to-all-start.9 = ((bf16[4,256,512]{1,2,0:T(8,128)(2,1)}), bf16[4,256,512]{1,2,0:T(8,128)(2,1)}, u32[]{:S(2)}, u32[]{:S(2)}) async-start(bf16[4,256,512]{1,2,0:T(8,128)(2,1)} %broadcast_in_dim.44), calls=%async_computation.9 | async-start | bytes 2097152 | tf_op jit(solution)/shard_map/all_to_all | solution.py:21
  197.7 1.2 copy.25
  198.9 13.7 %all-to-all-done.9 = bf16[4,256,512]{1,2,0:T(8,128)(2,1)} async-done(((bf16[4,256,512]{1,2,0:T(8,128)(2,1)}), bf16[4,256,512]{1,2,0:T(8,128)(2,1)}, u32[]{:S(2)}, u32[]{:S(2)}) %all-to-all-start.9) | async-done | bytes 1048608 | tf_op jit(solution)/shard_map/all_to_all | solution.py:21
  212.7 1.0 broadcast_in_dim.19
  213.7 4.2 %all-to-all-start.3 = ((bf16[4,256,512]{1,2,0:T(8,128)(2,1)}), bf16[4,256,512]{1,2,0:T(8,128)(2,1)}, u32[]{:S(2)}, u32[]{:S(2)}) async-start(bf16[4,256,512]{1,2,0:T(8,128)(2,1)} %broadcast_in_dim.19), calls=%async_computation.3 | async-start | bytes 2097152 | tf_op jit(solution)/shard_map/all_to_all | solution.py:21
  218.0 2.5 bitcast_convert_fusion
  220.5 1.0 copy.45
  221.5 11.5 %all-to-all-done.3 = bf16[4,256,512]{1,2,0:T(8,128)(2,1)} async-done(((bf16[4,256,512]{1,2,0:T(8,128)(2,1)}), bf16[4,256,512]{1,2,0:T(8,128)(2,1)}, u32[]{:S(2)}, u32[]{:S(2)}) %all-to-all-start.3) | async-done | bytes 1048608 | tf_op jit(solution)/shard_map/all_to_all | solution.py:21
  233.0 3.5 %all-to-all-start.10 = ((bf16[4,256,512]{1,2,0:T(8,128)(2,1)}), bf16[4,256,512]{1,2,0:T(8,128)(2,1)S(1)}, u32[]{:S(2)}, u32[]{:S(2)}) async-start(bf16[4,256,512]{1,2,0:T(8,128)(2,1)} %bitcast.75), calls=%async_computation.10 | async-start | bytes 2097152 | tf_op jit(solution)/shard_map/all_to_all | solution.py:21
  236.5 3.2 %bitcast_convert_fusion.1 = bf16[512,1024]{1,0:T(8,128)(2,1)S(1)} fusion(bf16[4,256,512]{1,2,0:T(8,128)(2,1)} %all-to-all-done.3, bf16[4,256,1024]{2,1,0:T(8,128)(2,1)} %copy-done), kind=kOutput, calls=%fused_computation.1 | convolution fusion | flops 1074266112 | bytes 4194304 | tf_op jit(solution)/shard_map/dot_general | solution.py:85
  239.7 1.0 copy.46
  240.7 20.9 %all-to-all-done.10 = bf16[4,256,512]{1,2,0:T(8,128)(2,1)S(1)} async-done(((bf16[4,256,512]{1,2,0:T(8,128)(2,1)}), bf16[4,256,512]{1,2,0:T(8,128)(2,1)S(1)}, u32[]{:S(2)}, u32[]{:S(2)}) %all-to-all-start.10) | async-done | bytes 1048608 | tf_op jit(solution)/shard_map/all_to_all | solution.py:21
  261.7 3.5 %all-to-all-start.4 = ((bf16[4,256,512]{1,2,0:T(8,128)(2,1)}), bf16[4,256,512]{1,2,0:T(8,128)(2,1)S(1)}, u32[]{:S(2)}, u32[]{:S(2)}) async-start(bf16[4,256,512]{1,2,0:T(8,128)(2,1)} %bitcast.76), calls=%async_computation.4 | async-start | bytes 2097152 | tf_op jit(solution)/shard_map/all_to_all | solution.py:21
  265.2 0.6 bitcast_dynamic-update-slice_fusion
  265.8 0.1 convert_bitcast_fusion
  266.0 0.1 copy.29
  266.1 0.9 fusion.3
  267.0 2.0 copy.39
  269.0 1.0 copy.40
  270.0 0.1 convert_reduce_fusion
  270.2 20.2 %all-to-all-done.4 = bf16[4,256,512]{1,2,0:T(8,128)(2,1)S(1)} async-done(((bf16[4,256,512]{1,2,0:T(8,128)(2,1)}), bf16[4,256,512]{1,2,0:T(8,128)(2,1)S(1)}, u32[]{:S(2)}, u32[]{:S(2)}) %all-to-all-start.4) | async-done | bytes 1048608 | tf_op jit(solution)/shard_map/all_to_all | solution.py:21
  290.4 0.1 convert_reduce_fusion.2
  290.5 1.4 add_multiply_fusion.1
  291.9 0.1 maximum_bitcast_fusion
  292.0 1.3 copy.36
  (21 shorter events, 0.1 us)
Async XLA Ops:
  5.0 29.2 %all-to-all-start.5 = ((bf16[16,2,8,1024]{3,2,1,0:T(8,128)(2,1)}), bf16[16,2,8,1024]{3,2,1,0:T(8,128)(2,1)S(1)}, u32[]{:S(2)}, u32[]{:S(2)}) async-start(bf16[16,2,8,1024]{3,2,1,0:T(8,128)(2,1)} %bitcast.13), calls=%async_computation.5 | async-start | bytes 1048576 | tf_op jit(solution)/shard_map/all_to_all | solution.py:21
  34.1 0.8 copy-start.3
  34.1 4.8 %copy-start.2 = (bf16[1,256,1024]{2,1,0:T(8,128)(2,1)S(1)}, bf16[1,256,1024]{2,1,0:T(8,128)(2,1)}, u32[]{:S(2)}) copy-start(bf16[1,256,1024]{2,1,0:T(8,128)(2,1)} %param.8) | copy-start | bytes 1572868
  34.9 30.2 %all-to-all-start = ((bf16[4,256,1024]{2,1,0:T(8,128)(2,1)}), bf16[4,256,1024]{2,1,0:T(8,128)(2,1)S(1)}, u32[]{:S(2)}, u32[]{:S(2)}) async-start(bf16[4,256,1024]{2,1,0:T(8,128)(2,1)} %bitcast.2), calls=%async_computation | async-start | bytes 4194304 | tf_op jit(solution)/shard_map/all_to_all | solution.py:21
  65.1 36.4 %copy-start = (bf16[4,256,1024]{2,1,0:T(8,128)(2,1)}, bf16[4,256,1024]{2,1,0:T(8,128)(2,1)S(1)}, u32[]{:S(2)}) copy-start(bf16[4,256,1024]{2,1,0:T(8,128)(2,1)S(1)} %all-to-all-done) | copy-start | bytes 6291460
  66.2 30.0 %all-to-all-start.7 = ((bf16[4,256,512]{2,1,0:T(8,128)(2,1)}), bf16[4,256,512]{2,1,0:T(8,128)(2,1)}, u32[]{:S(2)}, u32[]{:S(2)}) async-start(bf16[4,256,512]{2,1,0:T(8,128)(2,1)} %broadcast_in_dim.22), calls=%async_computation.7 | async-start | bytes 2097152 | tf_op jit(solution)/shard_map/all_to_all | solution.py:21
  97.2 29.5 %all-to-all-start.1 = ((bf16[4,256,512]{2,1,0:T(8,128)(2,1)}), bf16[4,256,512]{2,1,0:T(8,128)(2,1)}, u32[]{:S(2)}, u32[]{:S(2)}) async-start(bf16[4,256,512]{2,1,0:T(8,128)(2,1)} %broadcast_in_dim.18), calls=%async_computation.1 | async-start | bytes 2097152 | tf_op jit(solution)/shard_map/all_to_all | solution.py:21
  126.8 17.2 %all-to-all-start.8 = ((bf16[4,256,512]{2,1,0:T(8,128)(2,1)}), bf16[4,256,512]{2,1,0:T(8,128)(2,1)S(1)}, u32[]{:S(2)}, u32[]{:S(2)}) async-start(bf16[4,256,512]{2,1,0:T(8,128)(2,1)} %bitcast.89), calls=%async_computation.8 | async-start | bytes 2097152 | tf_op jit(solution)/shard_map/all_to_all | solution.py:21
  134.4 13.1 %copy-start.4 = (bf16[16,2,8,1024]{3,2,1,0:T(8,128)(2,1)S(1)}, bf16[16,2,8,1024]{3,2,1,0:T(8,128)(2,1)}, u32[]{:S(2)}) copy-start(bf16[16,2,8,1024]{3,2,1,0:T(8,128)(2,1)} %copy-done.3) | copy-start | bytes 1572868
  143.9 22.3 %all-to-all-start.2 = ((bf16[4,256,512]{2,1,0:T(8,128)(2,1)}), bf16[4,256,512]{2,1,0:T(8,128)(2,1)S(1)}, u32[]{:S(2)}, u32[]{:S(2)}) async-start(bf16[4,256,512]{2,1,0:T(8,128)(2,1)} %bitcast.88), calls=%async_computation.2 | async-start | bytes 2097152 | tf_op jit(solution)/shard_map/all_to_all | solution.py:21
  147.6 8.7 %collective-permute-start = (f32[8,1024]{1,0:T(8,128)S(1)}, f32[8,1024]{1,0:T(8,128)S(1)}, u32[]{:S(2)}, u32[]{:S(2)}) collective-permute-start(f32[8,1024]{1,0:T(8,128)S(1)} %dynamic-slice_bitcast_fusion), channel_id=1, source_target_pairs={{0,32},{32,0},{1,33},{33,1},{2,34},{34,2},{3,35},{35,3},{4,36},{36... | collective-permute-start | bytes 98312 | tf_op jit(solution)/shard_map/ppermute | solution.py:39
  157.7 8.5 %collective-permute-start.1 = (bf16[8,1024]{1,0:T(8,128)(2,1)S(1)}, bf16[8,1024]{1,0:T(8,128)(2,1)S(1)}, u32[]{:S(2)}, u32[]{:S(2)}) collective-permute-start(bf16[8,1024]{1,0:T(8,128)(2,1)S(1)} %get-tuple-element.6), channel_id=1, source_target_pairs={{0,32},{32,0},{1,33},{33,1},{2,34},{34,2},{3,35},{35,3},{4,36},{36... | collective-permute-start | bytes 49160 | tf_op jit(solution)/shard_map/ppermute | solution.py:49
  167.1 25.1 %all-to-all-start.6 = ((bf16[16,2,8,1024]{3,2,1,0:T(8,128)(2,1)}), bf16[16,2,8,1024]{3,2,1,0:T(8,128)(2,1)S(1)}, u32[]{:S(2)}, u32[]{:S(2)}) async-start(bf16[16,2,8,1024]{3,2,1,0:T(8,128)(2,1)} %broadcast_in_dim.20), calls=%async_computation.6 | async-start | bytes 1048576 | tf_op jit(solution)/shard_map/all_to_all | solution.py:21
  174.8 1.0 copy-start.5
  193.2 19.5 %all-to-all-start.9 = ((bf16[4,256,512]{1,2,0:T(8,128)(2,1)}), bf16[4,256,512]{1,2,0:T(8,128)(2,1)}, u32[]{:S(2)}, u32[]{:S(2)}) async-start(bf16[4,256,512]{1,2,0:T(8,128)(2,1)} %broadcast_in_dim.44), calls=%async_computation.9 | async-start | bytes 2097152 | tf_op jit(solution)/shard_map/all_to_all | solution.py:21
  197.7 20.3 %copy-start.1 = (bf16[4,256,1024]{2,1,0:T(8,128)(2,1)S(1)}, bf16[4,256,1024]{2,1,0:T(8,128)(2,1)}, u32[]{:S(2)}) copy-start(bf16[4,256,1024]{2,1,0:T(8,128)(2,1)} %copy-done) | copy-start | bytes 6291460
  213.7 19.3 %all-to-all-start.3 = ((bf16[4,256,512]{1,2,0:T(8,128)(2,1)}), bf16[4,256,512]{1,2,0:T(8,128)(2,1)}, u32[]{:S(2)}, u32[]{:S(2)}) async-start(bf16[4,256,512]{1,2,0:T(8,128)(2,1)} %broadcast_in_dim.19), calls=%async_computation.3 | async-start | bytes 2097152 | tf_op jit(solution)/shard_map/all_to_all | solution.py:21
  233.0 28.7 %all-to-all-start.10 = ((bf16[4,256,512]{1,2,0:T(8,128)(2,1)}), bf16[4,256,512]{1,2,0:T(8,128)(2,1)S(1)}, u32[]{:S(2)}, u32[]{:S(2)}) async-start(bf16[4,256,512]{1,2,0:T(8,128)(2,1)} %bitcast.75), calls=%async_computation.10 | async-start | bytes 2097152 | tf_op jit(solution)/shard_map/all_to_all | solution.py:21
  239.7 25.5 %copy-start.7 = (f32[8,1024]{1,0:T(8,128)S(1)}, f32[8,1024]{1,0:T(8,128)}, u32[]{:S(2)}) copy-start(f32[8,1024]{1,0:T(8,128)} %get-tuple-element.7) | copy-start | bytes 98308
  239.7 25.5 %copy-start.8 = (f32[8,1024]{1,0:T(8,128)S(1)}, f32[8,1024]{1,0:T(8,128)}, u32[]{:S(2)}) copy-start(f32[8,1024]{1,0:T(8,128)} %get-tuple-element.16) | copy-start | bytes 98308
  261.7 28.7 %all-to-all-start.4 = ((bf16[4,256,512]{1,2,0:T(8,128)(2,1)}), bf16[4,256,512]{1,2,0:T(8,128)(2,1)S(1)}, u32[]{:S(2)}, u32[]{:S(2)}) async-start(bf16[4,256,512]{1,2,0:T(8,128)(2,1)} %bitcast.76), calls=%async_computation.4 | async-start | bytes 2097152 | tf_op jit(solution)/shard_map/all_to_all | solution.py:21
  265.8 1.1 copy-start.6

commit v2 on v1

v2 whole, which is shorter than its diff:
```python
import functools

import jax
import jax.numpy as jnp
from jax import lax
from jax.experimental import pallas as pl
from jax.experimental.layout import Layout, with_layout_constraint
from jax.experimental.pallas import tpu as pltpu
from jax.sharding import Mesh, PartitionSpec as P

inner_rate = 1.0
outer_rate = 0.7
moment_keep = 0.9
merge_share = 0.5

PARTS = (("z", 8), ("yh", 2), ("core", 2), ("x", 4), ("yl", 4))
REPLICA = ("z", "yh", "core")
FSDP = ("x", "yl")
CUTS = (0, 384, 1024)
WIRE = jnp.float16
SHARE_UP = 32.0
GRAD_DOWN = 2.0**-8
EARLY = 30_000_000_000
VMEM_LIMIT = 12 << 20
VMEM = pl.BlockSpec(memory_space=pltpu.VMEM)
ANY = pl.BlockSpec(memory_space=pl.ANY)
SMEM = pl.BlockSpec(memory_space=pltpu.SMEM)


def exchange(blocks, axis):
    return lax.all_to_all(blocks, axis, 0, 0, tiled=True)


def rowwise(x):
    return with_layout_constraint(x, Layout(tuple(range(x.ndim))))


def shift(block, axis, s):
    n = lax.axis_size(axis)
    return lax.ppermute(block, axis, [(k, (k + s) % n) for k in range(n)])


def order_body(n, axis, at_ref, *refs):
    pieces, out = refs[:n], refs[n]
    for t in range(n):
        out[lax.rem(at_ref[axis] + (n - t), n)] = pieces[t][...]


def copy_body(at_ref, in_ref, out_ref):
    out_ref[...] = in_ref[...]


def split_body(n, tokens_ref, out_ref, done):
    width = tokens_ref.shape[1] // n
    copies = [
        pltpu.make_async_copy(tokens_ref.at[:, pl.ds(k * width, width)], out_ref.at[k], done.at[k]) for k in range(n)
    ]
    for copy in copies:
        copy.start()
    for copy in copies:
        copy.wait()


def on_vmem(body, outs, flops, moved, at, *operands, after=()):
    skip = len(after)

    def called(at_ref, *refs):
        body(at_ref, *refs[skip:])

    return pl.pallas_call(
        called,
        out_shape=outs,
        in_specs=[SMEM] + [ANY] * skip + [VMEM] * len(operands),
        out_specs=jax.tree.map(lambda _: VMEM, outs),
        compiler_params=pltpu.CompilerParams(vmem_limit_bytes=VMEM_LIMIT),
        cost_estimate=pl.CostEstimate(flops=flops, bytes_accessed=moved, transcendentals=0),
    )(at, *after, *operands)


def outer_body(replicas, at_ref, mine_ref, sent_ref, came_ref, params_ref, moment_ref, params_out, moment_out, pair_out):
    half, which = at_ref[2], at_ref[3]

    def step(g, m, summed):
        outer_grad = g - summed / replicas
        moment = moment_keep * m + outer_grad
        return g - outer_rate * (outer_grad + moment_keep * moment), moment

    here, moment = step(sent_ref[1], sent_ref[2], mine_ref[...] + came_ref[0])
    there, _ = step(came_ref[1], came_ref[2], came_ref[3] + sent_ref[0])
    params_out[...] = params_ref[...]
    moment_out[...] = moment_ref[...]
    params_out[which] = here
    moment_out[which] = moment
    pair_out[half] = here
    pair_out[1 - half] = there


def base_body(at_ref, rows_ref, spread_ref, out_ref):
    nz, nc, nh, piece, _ = spread_ref.shape
    for z in range(nz):
        for h in range(nh):
            for c in range(nc):
                first = ((z * nh + h) * nc + c) * piece
                own = rows_ref[pl.ds(first, piece), :]
                out_ref[pl.ds(first, piece), :] = merge_share * own + (1.0 - merge_share) * spread_ref[z, c, h]


def f32(*shape):
    return jax.ShapeDtypeStruct(shape, jnp.float32)


def on_device(inputs, targets, local_weight, outer_params, outer_moment, fragment):
    which = jnp.remainder(fragment[0], jnp.int32(outer_params.shape[0]))
    own_rows, tokens, wanted = local_weight[0], inputs[0], targets[0]
    rows, width = own_rows.shape
    count = tokens.shape[0]
    n = lax.axis_size("x")
    nz, nh, nc = (lax.axis_size(a) for a in REPLICA)
    piece = rows // (nz * nh * nc)
    half = lax.axis_index("yh")
    at = jnp.stack([lax.axis_index("x"), lax.axis_index("yl"), half, which]).astype(jnp.int32)
    features = tokens.shape[1] // n
    chunks = [slice(a, b) for a, b in zip(CUTS, CUTS[1:])]
    parts = [c.stop - c.start for c in chunks]
    last = len(chunks) - 1

    def hold(x, after):
        return on_vmem(copy_body, jax.ShapeDtypeStruct(x.shape, x.dtype), 0, x.size * 4, at, x, after=after)

    def in_order(pieces, axis, after=()):
        shape = (n,) + pieces[0].shape
        out = jax.ShapeDtypeStruct(shape, pieces[0].dtype)
        body = functools.partial(order_body, n, axis)
        return on_vmem(body, out, 0, 1 << 21, at, *pieces, after=after).reshape(n * shape[1], shape[2])

    blocks = pl.pallas_call(
        functools.partial(split_body, n),
        out_shape=jax.ShapeDtypeStruct((n, count, features), tokens.dtype),
        in_specs=[ANY],
        out_specs=VMEM,
        scratch_shapes=[pltpu.SemaphoreType.DMA((n,))],
        compiler_params=pltpu.CompilerParams(vmem_limit_bytes=VMEM_LIMIT),
    )(tokens)
    block = rowwise(exchange(blocks, "x").reshape(n * count, features))
    rows_now = hold(own_rows, [blocks])
    pieces = [[rows_now[:, c]] for c in chunks]
    for held in pieces:
        held.extend(shift(held[0], "yl", s) for s in range(1, n))
    weights = [in_order(pieces[0], 1, after=[pieces[1][1]])]

    core = lax.axis_index("core")
    by_owner = rows_now.reshape(nz, nh, nc, piece, width)
    sent = lax.dynamic_index_in_dim(by_owner, 1 - core, 2, keepdims=False)
    here = lax.dynamic_index_in_dim(by_owner, core, 2, keepdims=False).astype(jnp.float32)
    here = here + lax.ppermute(sent, "core", [(0, 1), (1, 0)]).astype(jnp.float32)
    part = lax.psum_scatter(here, "z", scatter_dimension=0, tiled=True)[0]

    part = on_vmem(copy_body, f32(*part.shape), EARLY, 1 << 18, at, part)

    def project(k):
        shares = jnp.dot(block, weights[k], preferred_element_type=jnp.float32)
        return rowwise((shares * SHARE_UP).astype(WIRE)).reshape(n, count, -1)

    def residual_of(got, aims):
        got = [got[k].astype(jnp.float32) for k in range(n)]
        projected = ((got[0] + got[1]) + (got[2] + got[3])) * (1.0 / SHARE_UP)
        return (projected - aims.astype(jnp.float32)).astype(jnp.bfloat16)

    def gradient(res):
        shares = lax.dot_general(
            block, rowwise(res.reshape(n * count, -1)), (((0,), (0,)), ((), ())), preferred_element_type=jnp.float32
        )
        return rowwise((shares * GRAD_DOWN).astype(WIRE)).reshape(n, rows, -1)

    whole = []
    for k, c in enumerate(chunks):
        aims = wanted[:, c] if k == 0 else hold(wanted[:, c], [residual])
        shares = project(k)
        if k < last:
            weights.append(in_order(pieces[k + 1], 1, after=[shares[0, :8, :128].astype(jnp.float32)]))
        residual = residual_of(exchange(shares, "x"), aims)
        if k == 0:
            residual = hold(residual, [part])
        whole.append(in_order([residual] + [shift(residual, "x", s) for s in range(1, n)], 0))

    g_piece = lax.dynamic_index_in_dim(outer_params, which, 0, keepdims=False)
    m_piece = lax.dynamic_index_in_dim(outer_moment, which, 0, keepdims=False)
    mine = lax.dynamic_index_in_dim(part, half, 0, keepdims=False)
    other = lax.dynamic_index_in_dim(part, 1 - half, 0, keepdims=False)
    sent = jnp.stack([other, g_piece, m_piece, mine])
    came = lax.ppermute(sent, "yh", [(0, 1), (1, 0)])
    new_params, new_moment, pair = on_vmem(
        functools.partial(outer_body, nz * nh * nc),
        [f32(*outer_params.shape), f32(*outer_moment.shape), f32(nh, piece, width)],
        0, 1 << 20, at, mine, sent, came, outer_params, outer_moment,
    )
    spread = lax.all_gather(pair, ("z", "core"), axis=0, tiled=False).reshape(nz, nc, nh, piece, width)

    gradients = []
    whole[0] = hold(whole[0], [pair])
    for k in range(last + 1):
        if k == last:
            base = on_vmem(base_body, f32(rows, width), 0, 1 << 22, at, own_rows.astype(jnp.float32), spread)
        got = exchange(gradient(whole[k]), "yl")
        got = [got[j].astype(jnp.float32) for j in range(n)]
        gradients.append((got[0] + got[1]) + (got[2] + got[3]))
    step = merge_share * inner_rate / (count * n * n * GRAD_DOWN)
    merged = base - step * jnp.concatenate(gradients, axis=1)
    return (merged[None], new_params, new_moment)


def solution(mesh):
    names = tuple(n for n, _ in PARTS)
    fine = Mesh(mesh.devices.reshape([k for _, k in PARTS]), names)
    local = P(REPLICA, FSDP, None)
    outer = P(None, FSDP + REPLICA, None)
    return jax.shard_map(
        on_device,
        mesh=fine,
        in_specs=(local, local, local, outer, outer, P()),
        out_specs=(local, outer, outer),
        check_vma=False,
    )
```

time: 295 us -> 202 us (0.68)
  waiting for transfers between devices: 177 us -> 62.9 us
  local copies, waits for them, and re-layouts: 26.7 us -> 10.7 us
  between operations: 1.58 us -> 15.1 us
  Pallas kernels: 0 us -> 8.9 us
  starting transfers between devices: 69.9 us -> 77.9 us
  matrix products: 13.2 us -> 16.5 us
    all_to_all x11 -> x5, waiting for transfers between devices: 176 us -> 2.78 us  [exchange(): return lax.all_to_all(blocks, axis, 0, 0, tiled=True)]
    ppermute x2 -> x14, starting transfers between devices: 14.7 us -> 50.2 us  [the longest x12 39.5 us: shift(): return lax.ppermute(block, axis, [(k, (k + s) % n) for k in range(n)])]
    ppermute x2 -> x14, waiting for transfers between devices: 1.83 us -> 34.3 us  [the longest x12 26.9 us: shift(): return lax.ppermute(block, axis, [(k, (k + s) % n) for k in range(n)])]
    all_to_all x11 -> x5, starting transfers between devices: 55.2 us -> 27.7 us  [exchange(): return lax.all_to_all(blocks, axis, 0, 0, tiled=True)]
    all_gather x0 -> x1, waiting for transfers between devices: none -> 25.7 us  [on_device(): lax.all_gather(pair, ('z', 'core'), axis=0, tiled=False)]
    pallas_call x0 -> x12, Pallas kernels: none -> 8.9 us  [the longest x11 7.33 us: on_vmem(): pl.pallas_call(called, out_shape=outs, in_specs=[SMEM] + [ANY] * skip + [...]
    broadcast_in_dim x5 -> x0, local copies, waits for them, and re-layouts: 5.1 us -> none  [gather(): return exchange(jnp.broadcast_to(block[None], (n,) + block.shape), axis)]
    dot_general x4, matrix products: 13.2 us -> 16.5 us  [the longest x2 8.33 us: gradient(): lax.dot_general(block, rowwise(res.reshape(n * count, -1)), (((0,), (0,))...]
  transfers between devices with their start and end apart: 13 -> 21, of which waited for: 12 -> 7; matrix products, arithmetic and copies ran while one was open for 10% -> 11% of each run, Pallas kernels for 0% -> 4%
where the time goes in v2:
time: 202 us; the launch traced here: 198 us
  starting transfers between devices  77.9 us (39%)
  waiting for transfers between devices  62.9 us (31%)
  matrix products  16.5 us (8%)
  between operations  15.1 us (7%)
  local copies, waits for them, and re-layouts  10.7 us (5%)
  Pallas kernels  8.9 us (4%)
  other arithmetic  6.11 us (3%)
    ppermute x12, starting transfers between devices, shift(): return lax.ppermute(block, axis, [(k, (k + s) % n) for k in range(n)])  39.5 us
    all_to_all x5, starting transfers between devices, exchange(): return lax.all_to_all(blocks, axis, 0, 0, tiled=True)  27.7 us
    ppermute x12, waiting for transfers between devices, shift(): return lax.ppermute(block, axis, [(k, (k + s) % n) for k in range(n)])  26.9 us
    all_gather x1, waiting for transfers between devices, on_device(): lax.all_gather(pair, ('z', 'core'), axis=0, tiled=False)  25.7 us
    unnamed x34, local copies, waits for them, and re-layouts  9.16 us
    ppermute x1, starting transfers between devices, on_device(): lax.ppermute(sent, 'core', [(0, 1), (1, 0)]).astype(jnp.float32)  8.57 us
    dot_general x2, matrix products, gradient(): lax.dot_general(block, rowwise(res.reshape(n * count, -1)), (((0,), (0,))...  8.33 us
    dot_general x2, matrix products, project(): shares = jnp.dot(block, weights[k], preferred_element_type=jnp.float32)  8.19 us
  transfers between devices with their start and end apart: 21, of which 7 were waited for; matrix products, arithmetic and copies ran while one was open for 11% of the time, Pallas kernels for 4%

profile of v2, /device:TPU:1, one launch (start us, length us, event | category | flops | bytes accessed | tf_op | source)
XLA Modules:
  0.0 198.1 jit_solution(16659248939420419207)
XLA Ops:
  7.2 1.6 copy-done
  8.8 1.6 shard_map.85.refs_0_
  10.3 5.0 %all-to-all-start = ((bf16[4,256,1024]{2,1,0:T(8,128)(2,1)}), bf16[4,256,1024]{2,1,0:T(8,128)(2,1)}, u32[]{:S(2)}, u32[]{:S(2)}) async-start(bf16[4,256,1024]{2,1,0:T(8,128)(2,1)} %shard_map.85.refs_0_), calls=%async_computation.1 | async-start | bytes 4194304 | tf_op jit(solution)/shard_map/all_to_all | solution.py:31
  16.0 0.1 pad_add_fusion.at_ref
  16.1 0.6 shard_map.86
  16.7 8.6 %collective-permute-start = (bf16[8,2,8,1024]{3,2,1,0:T(8,128)(2,1)S(1)}, bf16[8,2,8,1024]{3,2,1,0:T(8,128)(2,1)S(1)}, u32[]{:S(2)}, u32[]{:S(2)}) collective-permute-start(bf16[8,2,8,1024]{3,2,1,0:T(8,128)(2,1)S(1)} %dynamic-slice_bitcast_fusion), channel_id=1, source_target_pairs={{0,16},{16,0},{1,17},{17,1},{2,18},{18,2},{3,19},{19,3},{4,20},{20... | collective-permute-start | bytes 786440 | tf_op jit(solution)/shard_map/ppermute | solution.py:155
  25.3 1.9 collective-permute-start.3
  27.3 1.9 collective-permute-start.4
  29.2 5.2 %collective-permute-start.5 = (bf16[256,384]{1,0:T(8,128)(2,1)S(1)}, bf16[256,384]{1,0:T(8,128)(2,1)S(1)}, u32[]{:S(2)}, u32[]{:S(2)}) collective-permute-start(bf16[256,384]{1,0:T(8,128)(2,1)S(1)} %slice.85.refs_1_), channel_id=1, source_target_pairs={{0,3},{1,0},{2,1},{3,2},{4,7},{5,4},{6,5},{7,6},{8,11},{9,8},{10,9... | collective-permute-start | bytes 589832 | tf_op jit(solution)/shard_map/ppermute | solution.py:40
  34.4 2.2 %collective-permute-start.2 = (bf16[256,640]{1,0:T(8,128)(2,1)S(1)}, bf16[256,640]{1,0:T(8,128)(2,1)S(1)}, u32[]{:S(2)}, u32[]{:S(2)}) collective-permute-start(bf16[256,640]{1,0:T(8,128)(2,1)S(1)} %slice.84.refs_1_), channel_id=1, source_target_pairs={{0,1},{1,2},{2,3},{3,0},{4,5},{5,6},{6,7},{7,4},{8,9},{9,10},{10,1... | collective-permute-start | bytes 983048 | tf_op jit(solution)/shard_map/ppermute | solution.py:40
  36.6 4.9 %collective-permute-start.10 = (bf16[256,640]{1,0:T(8,128)(2,1)S(1)}, bf16[256,640]{1,0:T(8,128)(2,1)S(1)}, u32[]{:S(2)}, u32[]{:S(2)}) collective-permute-start(bf16[256,640]{1,0:T(8,128)(2,1)S(1)} %slice.84.refs_1_), channel_id=1, source_target_pairs={{0,3},{1,0},{2,1},{3,2},{4,7},{5,4},{6,5},{7,6},{8,11},{9,8},{10,9... | collective-permute-start | bytes 983048 | tf_op jit(solution)/shard_map/ppermute | solution.py:40
  41.5 0.9 convert_add_fusion
  42.5 1.4 constant_dynamic-slice_fusion
  43.8 0.7 copy-done.5
  44.5 1.9 collective-permute-start.9
  46.5 0.7 copy-done.7
  47.1 0.7 copy-done.9
  47.8 3.3 %collective-permute-done.2.refs_0_.refs_2_ = bf16[256,640]{1,0:T(8,128)(2,1)S(1)} collective-permute-done((bf16[256,640]{1,0:T(8,128)(2,1)S(1)}, bf16[256,640]{1,0:T(8,128)(2,1)S(1)}, u32[]{:S(2)}, u32[]{:S(2)}) %collective-permute-start.2) | collective-permute-done | bytes 327712 | tf_op jit(solution)/shard_map/ppermute | solution.py:40
  51.1 0.9 copy-done.6
  52.0 0.9 copy-done.8
  52.9 0.9 copy-done.10
  53.9 0.6 shard_map.90
  54.5 3.7 %multiply_convert_fusion.3 = f16[384,1024]{0,1:T(8,128)(2,1)} fusion(bf16[1024,1024]{1,0:T(8,128)(2,1)} %bitcast.14, bf16[1024,384]{1,0:T(8,128)(2,1)S(1)} %bitcast.75), kind=kOutput, calls=%fused_computation.3 | convolution fusion | flops 806092800 | bytes 3670016 | tf_op jit(solution)/shard_map/dot_general | solution.py:161
  58.2 4.4 %all-to-all-start.1 = ((f16[4,256,384]{2,1,0:T(8,128)(2,1)}), f16[4,256,384]{2,1,0:T(8,128)(2,1)S(1)}, u32[]{:S(2)}, u32[]{:S(2)}) async-start(f16[4,256,384]{2,1,0:T(8,128)(2,1)} %bitcast.78), calls=%async_computation.2 | async-start | bytes 1572864 | tf_op jit(solution)/shard_map/all_to_all | solution.py:31
  62.7 0.7 fusion.4.refs_0_
  63.3 13.3 %collective-permute-done.9.refs_3_ = bf16[256,640]{1,0:T(8,128)(2,1)S(1)} collective-permute-done((bf16[256,640]{1,0:T(8,128)(2,1)S(1)}, bf16[256,640]{1,0:T(8,128)(2,1)S(1)}, u32[]{:S(2)}, u32[]{:S(2)}) %collective-permute-start.9) | collective-permute-done | bytes 327712 | tf_op jit(solution)/shard_map/ppermute | solution.py:40
  76.7 0.6 shard_map.94
  77.3 4.5 %multiply_convert_fusion.1 = f16[640,1024]{0,1:T(8,128)(2,1)} fusion(bf16[1024,1024]{1,0:T(8,128)(2,1)} %bitcast.14, bf16[1024,640]{1,0:T(8,128)(2,1)S(1)} %bitcast.72), kind=kOutput, calls=%fused_computation.1 | convolution fusion | flops 1343488000 | bytes 4718592 | tf_op jit(solution)/shard_map/dot_general | solution.py:161
  81.8 4.4 %all-to-all-start.3 = ((f16[4,256,640]{2,1,0:T(8,128)(2,1)}), f16[4,256,640]{2,1,0:T(8,128)(2,1)}, u32[]{:S(2)}, u32[]{:S(2)}) async-start(f16[4,256,640]{2,1,0:T(8,128)(2,1)} %bitcast.27), calls=%async_computation.4 | async-start | bytes 2621440 | tf_op jit(solution)/shard_map/all_to_all | solution.py:31
  86.2 0.8 copy-done.11
  87.1 0.5 shard_map.87.refs_0_
  87.7 0.5 copy-done.13
  88.2 0.1 copy-done.14
  88.3 0.2 fusion.3.refs_1_
  88.5 0.6 shard_map.91.refs_0_
  89.1 3.5 %collective-permute-start.6 = (bf16[256,384]{1,0:T(8,128)(2,1)S(1)}, bf16[256,384]{1,0:T(8,128)(2,1)S(1)}, u32[]{:S(2)}, u32[]{:S(2)}) collective-permute-start(bf16[256,384]{1,0:T(8,128)(2,1)S(1)} %shard_map.91.refs_0_), channel_id=1, source_target_pairs={{0,4},{4,8},{8,12},{12,0},{1,5},{5,9},{9,13},{13,1},{2,6},{6,10},{... | collective-permute-start | bytes 589832 | tf_op jit(solution)/shard_map/ppermute | solution.py:40
  92.5 4.3 %collective-permute-start.7 = (bf16[256,384]{1,0:T(8,128)(2,1)S(1)}, bf16[256,384]{1,0:T(8,128)(2,1)S(1)}, u32[]{:S(2)}, u32[]{:S(2)}) collective-permute-start(bf16[256,384]{1,0:T(8,128)(2,1)S(1)} %shard_map.91.refs_0_), channel_id=1, source_target_pairs={{0,8},{4,12},{8,0},{12,4},{1,9},{5,13},{9,1},{13,5},{2,10},{6,14},... | collective-permute-start | bytes 589832 | tf_op jit(solution)/shard_map/ppermute | solution.py:40
  96.9 3.1 %collective-permute-start.8 = (bf16[256,384]{1,0:T(8,128)(2,1)S(1)}, bf16[256,384]{1,0:T(8,128)(2,1)S(1)}, u32[]{:S(2)}, u32[]{:S(2)}) collective-permute-start(bf16[256,384]{1,0:T(8,128)(2,1)S(1)} %shard_map.91.refs_0_), channel_id=1, source_target_pairs={{0,12},{4,0},{8,4},{12,8},{1,13},{5,1},{9,5},{13,9},{2,14},{6,2},{... | collective-permute-start | bytes 589832 | tf_op jit(solution)/shard_map/ppermute | solution.py:40
  100.0 2.2 %collective-permute-start.1 = (f32[4,8,1024]{2,1,0:T(8,128)S(1)}, f32[4,8,1024]{2,1,0:T(8,128)S(1)}, u32[]{:S(2)}, u32[]{:S(2)}) collective-permute-start(f32[4,8,1024]{2,1,0:T(8,128)S(1)} %pad_maximum_fusion.refs_1_), channel_id=1, source_target_pairs={{0,32},{32,0},{1,33},{33,1},{2,34},{34,2},{3,35},{35,3},{4,36},{36... | collective-permute-start | bytes 393224 | tf_op jit(solution)/shard_map/ppermute | solution.py:191
  102.2 7.5 %collective-permute-done.1.refs_2_ = f32[4,8,1024]{2,1,0:T(8,128)S(1)} collective-permute-done((f32[4,8,1024]{2,1,0:T(8,128)S(1)}, f32[4,8,1024]{2,1,0:T(8,128)S(1)}, u32[]{:S(2)}, u32[]{:S(2)}) %collective-permute-start.1) | collective-permute-done | bytes 131104 | tf_op jit(solution)/shard_map/ppermute | solution.py:191
  109.6 1.3 shard_map.88
  110.9 1.1 collective-permute-done.7.refs_2_
  112.1 0.6 shard_map.92
  112.7 0.6 shard_map.93
  113.3 3.8 %multiply_convert_fusion.2 = f16[384,1024]{0,1:T(8,128)(2,1)} fusion(bf16[1024,384]{1,0:T(8,128)(2,1)S(1)} %shard_map.93, bf16[1024,1024]{1,0:T(8,128)(2,1)} %bitcast.14), kind=kOutput, calls=%fused_computation.2 | convolution fusion | flops 806092800 | bytes 3670016 | tf_op jit(solution)/shard_map/dot_general | solution.py:170
  117.1 9.6 %all-to-all-start.2 = ((f16[4,256,384]{2,1,0:T(8,128)(2,1)}), f16[4,256,384]{2,1,0:T(8,128)(2,1)S(1)}, u32[]{:S(2)}, u32[]{:S(2)}) async-start(f16[4,256,384]{2,1,0:T(8,128)(2,1)} %bitcast.21), calls=%async_computation.3 | async-start | bytes 1572864 | tf_op jit(solution)/shard_map/all_to_all | solution.py:31
  126.7 0.6 shard_map.95
  127.3 1.5 fusion.2.refs_0_
  128.8 4.4 %collective-permute-start.11 = (bf16[256,640]{1,0:T(8,128)(2,1)S(1)}, bf16[256,640]{1,0:T(8,128)(2,1)S(1)}, u32[]{:S(2)}, u32[]{:S(2)}) collective-permute-start(bf16[256,640]{1,0:T(8,128)(2,1)S(1)} %fusion.2.refs_0_), channel_id=1, source_target_pairs={{0,4},{4,8},{8,12},{12,0},{1,5},{5,9},{9,13},{13,1},{2,6},{6,10},{... | collective-permute-start | bytes 983048 | tf_op jit(solution)/shard_map/ppermute | solution.py:40
  133.2 3.7 %collective-permute-start.12 = (bf16[256,640]{1,0:T(8,128)(2,1)S(1)}, bf16[256,640]{1,0:T(8,128)(2,1)S(1)}, u32[]{:S(2)}, u32[]{:S(2)}) collective-permute-start(bf16[256,640]{1,0:T(8,128)(2,1)S(1)} %fusion.2.refs_0_), channel_id=1, source_target_pairs={{0,8},{4,12},{8,0},{12,4},{1,9},{5,13},{9,1},{13,5},{2,10},{6,14},... | collective-permute-start | bytes 983048 | tf_op jit(solution)/shard_map/ppermute | solution.py:40
  136.9 2.5 %collective-permute-start.13 = (bf16[256,640]{1,0:T(8,128)(2,1)S(1)}, bf16[256,640]{1,0:T(8,128)(2,1)S(1)}, u32[]{:S(2)}, u32[]{:S(2)}) collective-permute-start(bf16[256,640]{1,0:T(8,128)(2,1)S(1)} %fusion.2.refs_0_), channel_id=1, source_target_pairs={{0,12},{4,0},{8,4},{12,8},{1,13},{5,1},{9,5},{13,9},{2,14},{6,2},{... | collective-permute-start | bytes 983048 | tf_op jit(solution)/shard_map/ppermute | solution.py:40
  139.4 0.0 all-gather.3.cloned.1.call-update
  139.5 9.1 %collective-permute-done.12.refs_2_ = bf16[256,640]{1,0:T(8,128)(2,1)S(1)} collective-permute-done((bf16[256,640]{1,0:T(8,128)(2,1)S(1)}, bf16[256,640]{1,0:T(8,128)(2,1)S(1)}, u32[]{:S(2)}, u32[]{:S(2)}) %collective-permute-start.12) | collective-permute-done | bytes 327712 | tf_op jit(solution)/shard_map/ppermute | solution.py:40
  148.6 0.7 shard_map.96
  149.2 4.5 %multiply_convert_fusion = f16[640,1024]{0,1:T(8,128)(2,1)} fusion(bf16[1024,640]{1,0:T(8,128)(2,1)S(1)} %bitcast.73, bf16[1024,1024]{1,0:T(8,128)(2,1)} %bitcast.14), kind=kOutput, calls=%fused_computation | convolution fusion | flops 1343488000 | bytes 4718592 | tf_op jit(solution)/shard_map/dot_general | solution.py:170
  153.8 4.3 %all-to-all-start.4 = ((f16[4,256,640]{2,1,0:T(8,128)(2,1)}), f16[4,256,640]{2,1,0:T(8,128)(2,1)}, u32[]{:S(2)}, u32[]{:S(2)}) async-start(f16[4,256,640]{2,1,0:T(8,128)(2,1)} %bitcast.31), calls=%async_computation.5 | async-start | bytes 2621440 | tf_op jit(solution)/shard_map/all_to_all | solution.py:31
  158.1 0.1 bitcast_convert_fusion.refs_0_
  158.2 25.7 %all-gather.3.cloned.1.call-done = f32[32,8,1024]{2,1,0:T(8,128)} async-done(((f32[2,8,1024]{2,1,0:T(8,128)}), f32[32,8,1024]{2,1,0:T(8,128)}) %all-gather.3.cloned.1.call-update) | async-done | bytes 1048592 | tf_op jit(solution)/shard_map/all_gather | solution.py:197
  183.9 1.2 copy-done.2
  185.1 0.7 shard_map.89
  185.8 0.1 add_bitcast_fusion.1
  185.9 2.8 %all-to-all-done.4 = f16[4,256,640]{2,1,0:T(8,128)(2,1)} async-done(((f16[4,256,640]{2,1,0:T(8,128)(2,1)}), f16[4,256,640]{2,1,0:T(8,128)(2,1)}, u32[]{:S(2)}, u32[]{:S(2)}) %all-to-all-start.4) | async-done | bytes 1310752 | tf_op jit(solution)/shard_map/all_to_all | solution.py:31
  188.7 1.4 add_bitcast_fusion
  190.1 1.1 fusion.1
  (46 shorter events, 0.3 us)
Async XLA Ops:
  7.2 1.6 copy-start
  10.3 5.8 %copy-start.1 = (bf16[1,256,1024]{2,1,0:T(8,128)(2,1)S(1)}, bf16[1,256,1024]{2,1,0:T(8,128)(2,1)}, u32[]{:S(2)}) copy-start(bf16[1,256,1024]{2,1,0:T(8,128)(2,1)} %param.8) | copy-start | bytes 1572868
  10.3 44.1 %all-to-all-start = ((bf16[4,256,1024]{2,1,0:T(8,128)(2,1)}), bf16[4,256,1024]{2,1,0:T(8,128)(2,1)}, u32[]{:S(2)}, u32[]{:S(2)}) async-start(bf16[4,256,1024]{2,1,0:T(8,128)(2,1)} %shard_map.85.refs_0_), calls=%async_computation.1 | async-start | bytes 4194304 | tf_op jit(solution)/shard_map/all_to_all | solution.py:31
  15.3 70.9 %reduce-scatter.2.cloned.1.call-start = ((), (), s32[]{:S(2)}) async-start(), calls=%async_computation.6 | async-start | bytes 589824 | tf_op jit(solution)/shard_map/reduce_scatter | solution.py:156
  16.7 25.8 %copy-start.3 = (f32[4,8,1024]{2,1,0:T(8,128)S(1)}, f32[4,8,1024]{2,1,0:T(8,128)}, u32[]{:S(2)}) copy-start(f32[4,8,1024]{2,1,0:T(8,128)} %refs_4_.1) | copy-start | bytes 393220
  16.7 19.9 %collective-permute-start = (bf16[8,2,8,1024]{3,2,1,0:T(8,128)(2,1)S(1)}, bf16[8,2,8,1024]{3,2,1,0:T(8,128)(2,1)S(1)}, u32[]{:S(2)}, u32[]{:S(2)}) collective-permute-start(bf16[8,2,8,1024]{3,2,1,0:T(8,128)(2,1)S(1)} %dynamic-slice_bitcast_fusion), channel_id=1, source_target_pairs={{0,16},{16,0},{1,17},{17,1},{2,18},{18,2},{3,19},{19,3},{4,20},{20... | collective-permute-start | bytes 786440 | tf_op jit(solution)/shard_map/ppermute | solution.py:155
  25.3 18.5 %collective-permute-start.3 = (bf16[256,384]{1,0:T(8,128)(2,1)S(1)}, bf16[256,384]{1,0:T(8,128)(2,1)S(1)}, u32[]{:S(2)}, u32[]{:S(2)}) collective-permute-start(bf16[256,384]{1,0:T(8,128)(2,1)S(1)} %slice.85.refs_1_), channel_id=1, source_target_pairs={{0,1},{1,2},{2,3},{3,0},{4,5},{5,6},{6,7},{7,4},{8,9},{9,10},{10,1... | collective-permute-start | bytes 589832 | tf_op jit(solution)/shard_map/ppermute | solution.py:40
  27.3 19.2 %collective-permute-start.4 = (bf16[256,384]{1,0:T(8,128)(2,1)S(1)}, bf16[256,384]{1,0:T(8,128)(2,1)S(1)}, u32[]{:S(2)}, u32[]{:S(2)}) collective-permute-start(bf16[256,384]{1,0:T(8,128)(2,1)S(1)} %slice.85.refs_1_), channel_id=1, source_target_pairs={{0,2},{1,3},{2,0},{3,1},{4,6},{5,7},{6,4},{7,5},{8,10},{9,11},{10,... | collective-permute-start | bytes 589832 | tf_op jit(solution)/shard_map/ppermute | solution.py:40
  29.2 18.0 %collective-permute-start.5 = (bf16[256,384]{1,0:T(8,128)(2,1)S(1)}, bf16[256,384]{1,0:T(8,128)(2,1)S(1)}, u32[]{:S(2)}, u32[]{:S(2)}) collective-permute-start(bf16[256,384]{1,0:T(8,128)(2,1)S(1)} %slice.85.refs_1_), channel_id=1, source_target_pairs={{0,3},{1,0},{2,1},{3,2},{4,7},{5,4},{6,5},{7,6},{8,11},{9,8},{10,9... | collective-permute-start | bytes 589832 | tf_op jit(solution)/shard_map/ppermute | solution.py:40
  34.4 16.7 %collective-permute-start.2 = (bf16[256,640]{1,0:T(8,128)(2,1)S(1)}, bf16[256,640]{1,0:T(8,128)(2,1)S(1)}, u32[]{:S(2)}, u32[]{:S(2)}) collective-permute-start(bf16[256,640]{1,0:T(8,128)(2,1)S(1)} %slice.84.refs_1_), channel_id=1, source_target_pairs={{0,1},{1,2},{2,3},{3,0},{4,5},{5,6},{6,7},{7,4},{8,9},{9,10},{10,1... | collective-permute-start | bytes 983048 | tf_op jit(solution)/shard_map/ppermute | solution.py:40
  36.6 26.7 %collective-permute-start.10 = (bf16[256,640]{1,0:T(8,128)(2,1)S(1)}, bf16[256,640]{1,0:T(8,128)(2,1)S(1)}, u32[]{:S(2)}, u32[]{:S(2)}) collective-permute-start(bf16[256,640]{1,0:T(8,128)(2,1)S(1)} %slice.84.refs_1_), channel_id=1, source_target_pairs={{0,3},{1,0},{2,1},{3,2},{4,7},{5,4},{6,5},{7,6},{8,11},{9,8},{10,9... | collective-permute-start | bytes 983048 | tf_op jit(solution)/shard_map/ppermute | solution.py:40
  43.8 0.7 copy-start.5
  44.5 32.1 %collective-permute-start.9 = (bf16[256,640]{1,0:T(8,128)(2,1)S(1)}, bf16[256,640]{1,0:T(8,128)(2,1)S(1)}, u32[]{:S(2)}, u32[]{:S(2)}) collective-permute-start(bf16[256,640]{1,0:T(8,128)(2,1)S(1)} %slice.84.refs_1_), channel_id=1, source_target_pairs={{0,2},{1,3},{2,0},{3,1},{4,6},{5,7},{6,4},{7,5},{8,10},{9,11},{10,... | collective-permute-start | bytes 983048 | tf_op jit(solution)/shard_map/ppermute | solution.py:40
  46.5 0.7 copy-start.7
  47.1 0.7 copy-start.9
  51.1 0.9 copy-start.6
  52.0 0.9 copy-start.8
  52.9 0.9 copy-start.10
  58.2 23.6 %all-to-all-start.1 = ((f16[4,256,384]{2,1,0:T(8,128)(2,1)}), f16[4,256,384]{2,1,0:T(8,128)(2,1)S(1)}, u32[]{:S(2)}, u32[]{:S(2)}) async-start(f16[4,256,384]{2,1,0:T(8,128)(2,1)} %bitcast.78), calls=%async_computation.2 | async-start | bytes 1572864 | tf_op jit(solution)/shard_map/all_to_all | solution.py:31
  81.8 4.4 %copy-start.12 = (f16[4,256,384]{2,1,0:T(8,128)(2,1)}, f16[4,256,384]{2,1,0:T(8,128)(2,1)S(1)}, u32[]{:S(2)}) copy-start(f16[4,256,384]{2,1,0:T(8,128)(2,1)S(1)} %all-to-all-done.1) | copy-start | bytes 2359300
  81.8 35.3 %all-to-all-start.3 = ((f16[4,256,640]{2,1,0:T(8,128)(2,1)}), f16[4,256,640]{2,1,0:T(8,128)(2,1)}, u32[]{:S(2)}, u32[]{:S(2)}) async-start(f16[4,256,640]{2,1,0:T(8,128)(2,1)} %bitcast.27), calls=%async_computation.4 | async-start | bytes 2621440 | tf_op jit(solution)/shard_map/all_to_all | solution.py:31
  86.2 0.8 copy-start.11
  87.1 1.1 copy-start.13
  87.1 1.3 copy-start.14
  87.6 12.3 %copy-start.15 = (f32[1,8,1024]{2,1,0:T(8,128)S(1)}, f32[1,8,1024]{2,1,0:T(8,128)}, u32[]{:S(2)}) copy-start(f32[1,8,1024]{2,1,0:T(8,128)} %get-tuple-element.11) | copy-start | bytes 98308
  87.6 12.3 %copy-start.16 = (f32[1,8,1024]{2,1,0:T(8,128)S(1)}, f32[1,8,1024]{2,1,0:T(8,128)}, u32[]{:S(2)}) copy-start(f32[1,8,1024]{2,1,0:T(8,128)} %get-tuple-element.12) | copy-start | bytes 98308
  87.7 22.0 %copy-start.4 = (f32[4,8,1024]{2,1,0:T(8,128)S(1)}, f32[4,8,1024]{2,1,0:T(8,128)}, u32[]{:S(2)}) copy-start(f32[4,8,1024]{2,1,0:T(8,128)} %refs_3_.1) | copy-start | bytes 393220
  89.1 21.8 %collective-permute-start.6 = (bf16[256,384]{1,0:T(8,128)(2,1)S(1)}, bf16[256,384]{1,0:T(8,128)(2,1)S(1)}, u32[]{:S(2)}, u32[]{:S(2)}) collective-permute-start(bf16[256,384]{1,0:T(8,128)(2,1)S(1)} %shard_map.91.refs_0_), channel_id=1, source_target_pairs={{0,4},{4,8},{8,12},{12,0},{1,5},{5,9},{9,13},{13,1},{2,6},{6,10},{... | collective-permute-start | bytes 589832 | tf_op jit(solution)/shard_map/ppermute | solution.py:40
  92.5 19.5 %collective-permute-start.7 = (bf16[256,384]{1,0:T(8,128)(2,1)S(1)}, bf16[256,384]{1,0:T(8,128)(2,1)S(1)}, u32[]{:S(2)}, u32[]{:S(2)}) collective-permute-start(bf16[256,384]{1,0:T(8,128)(2,1)S(1)} %shard_map.91.refs_0_), channel_id=1, source_target_pairs={{0,8},{4,12},{8,0},{12,4},{1,9},{5,13},{9,1},{13,5},{2,10},{6,14},... | collective-permute-start | bytes 589832 | tf_op jit(solution)/shard_map/ppermute | solution.py:40
  96.9 15.2 %collective-permute-start.8 = (bf16[256,384]{1,0:T(8,128)(2,1)S(1)}, bf16[256,384]{1,0:T(8,128)(2,1)S(1)}, u32[]{:S(2)}, u32[]{:S(2)}) collective-permute-start(bf16[256,384]{1,0:T(8,128)(2,1)S(1)} %shard_map.91.refs_0_), channel_id=1, source_target_pairs={{0,12},{4,0},{8,4},{12,8},{1,13},{5,1},{9,5},{13,9},{2,14},{6,2},{... | collective-permute-start | bytes 589832 | tf_op jit(solution)/shard_map/ppermute | solution.py:40
  100.0 9.6 %collective-permute-start.1 = (f32[4,8,1024]{2,1,0:T(8,128)S(1)}, f32[4,8,1024]{2,1,0:T(8,128)S(1)}, u32[]{:S(2)}, u32[]{:S(2)}) collective-permute-start(f32[4,8,1024]{2,1,0:T(8,128)S(1)} %pad_maximum_fusion.refs_1_), channel_id=1, source_target_pairs={{0,32},{32,0},{1,33},{33,1},{2,34},{34,2},{3,35},{35,3},{4,36},{36... | collective-permute-start | bytes 393224 | tf_op jit(solution)/shard_map/ppermute | solution.py:191
  117.1 36.7 %all-to-all-start.2 = ((f16[4,256,384]{2,1,0:T(8,128)(2,1)}), f16[4,256,384]{2,1,0:T(8,128)(2,1)S(1)}, u32[]{:S(2)}, u32[]{:S(2)}) async-start(f16[4,256,384]{2,1,0:T(8,128)(2,1)} %bitcast.21), calls=%async_computation.3 | async-start | bytes 1572864 | tf_op jit(solution)/shard_map/all_to_all | solution.py:31
  126.6 57.3 %all-gather.3.cloned.1.call-start = ((), (), s32[]{:S(2)}) async-start(), calls=%async_computation.7 | async-start | bytes 1114112 | tf_op jit(solution)/shard_map/all_gather | solution.py:197
  128.8 10.7 %collective-permute-start.11 = (bf16[256,640]{1,0:T(8,128)(2,1)S(1)}, bf16[256,640]{1,0:T(8,128)(2,1)S(1)}, u32[]{:S(2)}, u32[]{:S(2)}) collective-permute-start(bf16[256,640]{1,0:T(8,128)(2,1)S(1)} %fusion.2.refs_0_), channel_id=1, source_target_pairs={{0,4},{4,8},{8,12},{12,0},{1,5},{5,9},{9,13},{13,1},{2,6},{6,10},{... | collective-permute-start | bytes 983048 | tf_op jit(solution)/shard_map/ppermute | solution.py:40
  133.2 15.4 %collective-permute-start.12 = (bf16[256,640]{1,0:T(8,128)(2,1)S(1)}, bf16[256,640]{1,0:T(8,128)(2,1)S(1)}, u32[]{:S(2)}, u32[]{:S(2)}) collective-permute-start(bf16[256,640]{1,0:T(8,128)(2,1)S(1)} %fusion.2.refs_0_), channel_id=1, source_target_pairs={{0,8},{4,12},{8,0},{12,4},{1,9},{5,13},{9,1},{13,5},{2,10},{6,14},... | collective-permute-start | bytes 983048 | tf_op jit(solution)/shard_map/ppermute | solution.py:40
  136.9 11.7 %collective-permute-start.13 = (bf16[256,640]{1,0:T(8,128)(2,1)S(1)}, bf16[256,640]{1,0:T(8,128)(2,1)S(1)}, u32[]{:S(2)}, u32[]{:S(2)}) collective-permute-start(bf16[256,640]{1,0:T(8,128)(2,1)S(1)} %fusion.2.refs_0_), channel_id=1, source_target_pairs={{0,12},{4,0},{8,4},{12,8},{1,13},{5,1},{9,5},{13,9},{2,14},{6,2},{... | collective-permute-start | bytes 983048 | tf_op jit(solution)/shard_map/ppermute | solution.py:40
  153.8 34.9 %all-to-all-start.4 = ((f16[4,256,640]{2,1,0:T(8,128)(2,1)}), f16[4,256,640]{2,1,0:T(8,128)(2,1)}, u32[]{:S(2)}, u32[]{:S(2)}) async-start(f16[4,256,640]{2,1,0:T(8,128)(2,1)} %bitcast.31), calls=%async_computation.5 | async-start | bytes 2621440 | tf_op jit(solution)/shard_map/all_to_all | solution.py:31
  183.9 1.2 copy-start.2
Sparse Core Ops, SparseCore 0:
  42.6 35.9 reduce-scatter.1
  139.6 44.2 all-gather.2

commit v3 on v2

--- a/solution.py
+++ b/solution.py
@@ -16,7 +16,7 @@
 PARTS = (("z", 8), ("yh", 2), ("core", 2), ("x", 4), ("yl", 4))
 REPLICA = ("z", "yh", "core")
 FSDP = ("x", "yl")
-CUTS = (0, 384, 1024)
+CUTS = (0, 512, 1024)
 WIRE = jnp.float16
 SHARE_UP = 32.0
 GRAD_DOWN = 2.0**-8
@@ -197,7 +197,7 @@
     spread = lax.all_gather(pair, ("z", "core"), axis=0, tiled=False).reshape(nz, nc, nh, piece, width)
 
     gradients = []
-    whole[0] = hold(whole[0], [pair])
+    whole[0] = hold(whole[0], [came])
     for k in range(last + 1):
         if k == last:
             base = on_vmem(base_body, f32(rows, width), 0, 1 << 22, at, own_rows.astype(jnp.float32), spread)

time: 202 us -> 192 us (0.950)
  local copies, waits for them, and re-layouts: 10.7 us -> 5.16 us
  starting transfers between devices: 77.9 us -> 73.6 us
    ppermute x12, waiting for transfers between devices: 26.9 us -> 39.2 us  [shift(): return lax.ppermute(block, axis, [(k, (k + s) % n) for k in range(n)])]
    ppermute x1, waiting for transfers between devices: 7.46 us -> 0.01 us  [on_device(): came = lax.ppermute(sent, 'yh', [(0, 1), (1, 0)])]
    unnamed x34 -> x18, local copies, waits for them, and re-layouts: 9.16 us -> 3.68 us
    all_to_all x5, starting transfers between devices: 27.7 us -> 22.8 us  [exchange(): return lax.all_to_all(blocks, axis, 0, 0, tiled=True)]
    all_gather x1, waiting for transfers between devices: 25.7 us -> 21.1 us  [on_device(): lax.all_gather(pair, ('z', 'core'), axis=0, tiled=False)]
  transfers between devices with their start and end apart: 21 -> 21, of which waited for: 7 -> 9; matrix products, arithmetic and copies ran while one was open for 11% -> 11% of each run, Pallas kernels for 4% -> 4%
where the time goes in v3:
time: 192 us; the launch traced here: 188 us
  starting transfers between devices  73.6 us (38%)
  waiting for transfers between devices  62.4 us (32%)
  matrix products  15.4 us (8%)
  between operations  15.1 us (8%)
  Pallas kernels  9.24 us (5%)
  other arithmetic  6.87 us (4%)
  local copies, waits for them, and re-layouts  5.16 us (3%)
    ppermute x12, starting transfers between devices, shift(): return lax.ppermute(block, axis, [(k, (k + s) % n) for k in range(n)])  40.1 us
    ppermute x12, waiting for transfers between devices, shift(): return lax.ppermute(block, axis, [(k, (k + s) % n) for k in range(n)])  39.2 us
    all_to_all x5, starting transfers between devices, exchange(): return lax.all_to_all(blocks, axis, 0, 0, tiled=True)  22.8 us
    all_gather x1, waiting for transfers between devices, on_device(): lax.all_gather(pair, ('z', 'core'), axis=0, tiled=False)  21.1 us
    ppermute x1, starting transfers between devices, on_device(): lax.ppermute(sent, 'core', [(0, 1), (1, 0)]).astype(jnp.float32)  8.58 us
    dot_general x2, matrix products, gradient(): lax.dot_general(block, rowwise(res.reshape(n * count, -1)), (((0,), (0,))...  7.8 us
    pallas_call x11, Pallas kernels, on_vmem(): pl.pallas_call(called, out_shape=outs, in_specs=[SMEM] + [ANY] * skip + [...  7.67 us
    dot_general x2, matrix products, project(): shares = jnp.dot(block, weights[k], preferred_element_type=jnp.float32)  7.65 us
  transfers between devices with their start and end apart: 21, of which 9 were waited for; matrix products, arithmetic and copies ran while one was open for 11% of the time, Pallas kernels for 4%

profile of v3, /device:TPU:1, one launch (start us, length us, event | category | flops | bytes accessed | tf_op | source)
XLA Modules:
  0.0 187.8 jit_solution(14618913384588375819)
XLA Ops:
  7.2 1.6 copy-done
  8.8 1.6 shard_map.85.refs_0_
  10.3 0.0 copy-start.1
  10.3 5.0 %all-to-all-start = ((bf16[4,256,1024]{2,1,0:T(8,128)(2,1)}), bf16[4,256,1024]{2,1,0:T(8,128)(2,1)}, u32[]{:S(2)}, u32[]{:S(2)}) async-start(bf16[4,256,1024]{2,1,0:T(8,128)(2,1)} %shard_map.85.refs_0_), calls=%async_computation.1 | async-start | bytes 4194304 | tf_op jit(solution)/shard_map/all_to_all | solution.py:31
  16.0 0.1 pad_add_fusion.at_ref
  16.1 0.6 shard_map.86
  16.7 0.0 copy-start.3
  16.7 8.6 %collective-permute-start = (bf16[8,2,8,1024]{3,2,1,0:T(8,128)(2,1)S(1)}, bf16[8,2,8,1024]{3,2,1,0:T(8,128)(2,1)S(1)}, u32[]{:S(2)}, u32[]{:S(2)}) collective-permute-start(bf16[8,2,8,1024]{3,2,1,0:T(8,128)(2,1)S(1)} %dynamic-slice_bitcast_fusion), channel_id=1, source_target_pairs={{0,16},{16,0},{1,17},{17,1},{2,18},{18,2},{3,19},{19,3},{4,20},{20... | collective-permute-start | bytes 786440 | tf_op jit(solution)/shard_map/ppermute | solution.py:155
  25.3 1.1 collective-permute-done
  26.4 0.9 convert_add_fusion
  27.3 0.0 reduce-scatter.2.cloned.1.call-update
  27.4 1.9 %collective-permute-start.2 = (bf16[256,512]{1,0:T(8,128)(2,1)S(1)}, bf16[256,512]{1,0:T(8,128)(2,1)S(1)}, u32[]{:S(2)}, u32[]{:S(2)}) collective-permute-start(bf16[256,512]{1,0:T(8,128)(2,1)S(1)} %get-tuple-element.10.refs_1_), channel_id=1, source_target_pairs={{0,1},{1,2},{2,3},{3,0},{4,5},{5,6},{6,7},{7,4},{8,9},{9,10},{10,1... | collective-permute-start | bytes 786440 | tf_op jit(solution)/shard_map/ppermute | solution.py:40
  29.3 1.9 %collective-permute-start.3 = (bf16[256,512]{1,0:T(8,128)(2,1)S(1)}, bf16[256,512]{1,0:T(8,128)(2,1)S(1)}, u32[]{:S(2)}, u32[]{:S(2)}) collective-permute-start(bf16[256,512]{1,0:T(8,128)(2,1)S(1)} %get-tuple-element.9.refs_1_), channel_id=1, source_target_pairs={{0,1},{1,2},{2,3},{3,0},{4,5},{5,6},{6,7},{7,4},{8,9},{9,10},{10,1... | collective-permute-start | bytes 786440 | tf_op jit(solution)/shard_map/ppermute | solution.py:40
  31.2 5.4 %collective-permute-start.4 = (bf16[256,512]{1,0:T(8,128)(2,1)S(1)}, bf16[256,512]{1,0:T(8,128)(2,1)S(1)}, u32[]{:S(2)}, u32[]{:S(2)}) collective-permute-start(bf16[256,512]{1,0:T(8,128)(2,1)S(1)} %get-tuple-element.9.refs_1_), channel_id=1, source_target_pairs={{0,2},{1,3},{2,0},{3,1},{4,6},{5,7},{6,4},{7,5},{8,10},{9,11},{10,... | collective-permute-start | bytes 786440 | tf_op jit(solution)/shard_map/ppermute | solution.py:40
  36.7 1.9 %collective-permute-start.5 = (bf16[256,512]{1,0:T(8,128)(2,1)S(1)}, bf16[256,512]{1,0:T(8,128)(2,1)S(1)}, u32[]{:S(2)}, u32[]{:S(2)}) collective-permute-start(bf16[256,512]{1,0:T(8,128)(2,1)S(1)} %get-tuple-element.9.refs_1_), channel_id=1, source_target_pairs={{0,3},{1,0},{2,1},{3,2},{4,7},{5,4},{6,5},{7,6},{8,11},{9,8},{10,9... | collective-permute-start | bytes 786440 | tf_op jit(solution)/shard_map/ppermute | solution.py:40
  38.6 3.1 %collective-permute-start.10 = (bf16[256,512]{1,0:T(8,128)(2,1)S(1)}, bf16[256,512]{1,0:T(8,128)(2,1)S(1)}, u32[]{:S(2)}, u32[]{:S(2)}) collective-permute-start(bf16[256,512]{1,0:T(8,128)(2,1)S(1)} %get-tuple-element.10.refs_1_), channel_id=1, source_target_pairs={{0,3},{1,0},{2,1},{3,2},{4,7},{5,4},{6,5},{7,6},{8,11},{9,8},{10,9... | collective-permute-start | bytes 786440 | tf_op jit(solution)/shard_map/ppermute | solution.py:40
  41.7 1.4 constant_dynamic-slice_fusion
  43.1 3.4 %collective-permute-start.9 = (bf16[256,512]{1,0:T(8,128)(2,1)S(1)}, bf16[256,512]{1,0:T(8,128)(2,1)}, u32[]{:S(2)}, u32[]{:S(2)}) collective-permute-start(bf16[256,512]{1,0:T(8,128)(2,1)S(1)} %get-tuple-element.10.refs_1_), channel_id=1, source_target_pairs={{0,2},{1,3},{2,0},{3,1},{4,6},{5,7},{6,4},{7,5},{8,10},{9,11},{10,... | collective-permute-start | bytes 786440 | tf_op jit(solution)/shard_map/ppermute | solution.py:40
  46.5 0.0 collective-permute-done.3.refs_2_
  46.5 9.8 %collective-permute-done.4.refs_3_ = bf16[256,512]{1,0:T(8,128)(2,1)S(1)} collective-permute-done((bf16[256,512]{1,0:T(8,128)(2,1)S(1)}, bf16[256,512]{1,0:T(8,128)(2,1)S(1)}, u32[]{:S(2)}, u32[]{:S(2)}) %collective-permute-start.4) | collective-permute-done | bytes 262176 | tf_op jit(solution)/shard_map/ppermute | solution.py:40
  56.3 0.0 collective-permute-done.5.refs_4_
  56.3 0.6 shard_map.90
  56.9 3.8 %multiply_convert_fusion.3 = f16[512,1024]{0,1:T(8,128)(2,1)} fusion(bf16[1024,1024]{1,0:T(8,128)(2,1)} %bitcast.14, bf16[1024,512]{1,0:T(8,128)(2,1)S(1)} %bitcast.72), kind=kOutput, calls=%fused_computation.3 | convolution fusion | flops 1074790400 | bytes 4194304 | tf_op jit(solution)/shard_map/dot_general | solution.py:161
  60.8 4.4 %all-to-all-start.1 = ((f16[4,256,512]{2,1,0:T(8,128)(2,1)}), f16[4,256,512]{2,1,0:T(8,128)(2,1)S(1)}, u32[]{:S(2)}, u32[]{:S(2)}) async-start(f16[4,256,512]{2,1,0:T(8,128)(2,1)} %bitcast.78), calls=%async_computation.2 | async-start | bytes 2097152 | tf_op jit(solution)/shard_map/all_to_all | solution.py:31
  65.1 0.8 copy-done.5
  66.0 0.5 shard_map.87.refs_0_
  66.5 0.7 fusion.4.refs_0_
  67.2 11.6 %collective-permute-done.9.refs_3_ = bf16[256,512]{1,0:T(8,128)(2,1)} collective-permute-done((bf16[256,512]{1,0:T(8,128)(2,1)S(1)}, bf16[256,512]{1,0:T(8,128)(2,1)}, u32[]{:S(2)}, u32[]{:S(2)}) %collective-permute-start.9) | collective-permute-done | bytes 262176 | tf_op jit(solution)/shard_map/ppermute | solution.py:40
  78.8 1.0 shard_map.94
  79.8 3.8 %multiply_convert_fusion.1 = f16[512,1024]{0,1:T(8,128)(2,1)} fusion(bf16[1024,1024]{1,0:T(8,128)(2,1)} %bitcast.14, bf16[1024,512]{1,0:T(8,128)(2,1)S(1)} %bitcast.73), kind=kOutput, calls=%fused_computation.1 | convolution fusion | flops 1074790400 | bytes 4194304 | tf_op jit(solution)/shard_map/dot_general | solution.py:161
  83.7 4.6 %all-to-all-start.3 = ((f16[4,256,512]{2,1,0:T(8,128)(2,1)}), f16[4,256,512]{2,1,0:T(8,128)(2,1)S(1)}, u32[]{:S(2)}, u32[]{:S(2)}) async-start(f16[4,256,512]{2,1,0:T(8,128)(2,1)} %bitcast.81), calls=%async_computation.4 | async-start | bytes 2097152 | tf_op jit(solution)/shard_map/all_to_all | solution.py:31
  88.2 1.2 fusion.3.refs_1_
  89.4 0.6 shard_map.91.refs_0_
  90.0 3.4 %collective-permute-start.6 = (bf16[256,512]{1,0:T(8,128)(2,1)S(1)}, bf16[256,512]{1,0:T(8,128)(2,1)S(1)}, u32[]{:S(2)}, u32[]{:S(2)}) collective-permute-start(bf16[256,512]{1,0:T(8,128)(2,1)S(1)} %shard_map.91.refs_0_), channel_id=1, source_target_pairs={{0,4},{4,8},{8,12},{12,0},{1,5},{5,9},{9,13},{13,1},{2,6},{6,10},{... | collective-permute-start | bytes 786440 | tf_op jit(solution)/shard_map/ppermute | solution.py:40
  93.4 4.3 %collective-permute-start.7 = (bf16[256,512]{1,0:T(8,128)(2,1)S(1)}, bf16[256,512]{1,0:T(8,128)(2,1)S(1)}, u32[]{:S(2)}, u32[]{:S(2)}) collective-permute-start(bf16[256,512]{1,0:T(8,128)(2,1)S(1)} %shard_map.91.refs_0_), channel_id=1, source_target_pairs={{0,8},{4,12},{8,0},{12,4},{1,9},{5,13},{9,1},{13,5},{2,10},{6,14},... | collective-permute-start | bytes 786440 | tf_op jit(solution)/shard_map/ppermute | solution.py:40
  97.7 3.1 %collective-permute-start.8 = (bf16[256,512]{1,0:T(8,128)(2,1)S(1)}, bf16[256,512]{1,0:T(8,128)(2,1)S(1)}, u32[]{:S(2)}, u32[]{:S(2)}) collective-permute-start(bf16[256,512]{1,0:T(8,128)(2,1)S(1)} %shard_map.91.refs_0_), channel_id=1, source_target_pairs={{0,12},{4,0},{8,4},{12,8},{1,13},{5,1},{9,5},{13,9},{2,14},{6,2},{... | collective-permute-start | bytes 786440 | tf_op jit(solution)/shard_map/ppermute | solution.py:40
  100.8 2.1 %collective-permute-start.1 = (f32[4,8,1024]{2,1,0:T(8,128)S(1)}, f32[4,8,1024]{2,1,0:T(8,128)S(1)}, u32[]{:S(2)}, u32[]{:S(2)}) collective-permute-start(f32[4,8,1024]{2,1,0:T(8,128)S(1)} %pad_maximum_fusion.refs_1_), channel_id=1, source_target_pairs={{0,32},{32,0},{1,33},{33,1},{2,34},{34,2},{3,35},{35,3},{4,36},{36... | collective-permute-start | bytes 393224 | tf_op jit(solution)/shard_map/ppermute | solution.py:191
  102.9 5.0 %collective-permute-done.6.refs_1_ = bf16[256,512]{1,0:T(8,128)(2,1)S(1)} collective-permute-done((bf16[256,512]{1,0:T(8,128)(2,1)S(1)}, bf16[256,512]{1,0:T(8,128)(2,1)S(1)}, u32[]{:S(2)}, u32[]{:S(2)}) %collective-permute-start.6) | collective-permute-done | bytes 262176 | tf_op jit(solution)/shard_map/ppermute | solution.py:40
  108.0 6.0 %collective-permute-done.7.refs_2_ = bf16[256,512]{1,0:T(8,128)(2,1)S(1)} collective-permute-done((bf16[256,512]{1,0:T(8,128)(2,1)S(1)}, bf16[256,512]{1,0:T(8,128)(2,1)S(1)}, u32[]{:S(2)}, u32[]{:S(2)}) %collective-permute-start.7) | collective-permute-done | bytes 262176 | tf_op jit(solution)/shard_map/ppermute | solution.py:40
  113.9 0.6 shard_map.92
  114.6 0.6 shard_map.93
  115.2 3.9 %multiply_convert_fusion.2 = f16[512,1024]{0,1:T(8,128)(2,1)} fusion(bf16[1024,512]{1,0:T(8,128)(2,1)S(1)} %shard_map.93, bf16[1024,1024]{1,0:T(8,128)(2,1)} %bitcast.14), kind=kOutput, calls=%fused_computation.2 | convolution fusion | flops 1074790400 | bytes 4194304 | tf_op jit(solution)/shard_map/dot_general | solution.py:170
  119.1 4.4 %all-to-all-start.2 = ((f16[4,256,512]{2,1,0:T(8,128)(2,1)}), f16[4,256,512]{2,1,0:T(8,128)(2,1)}, u32[]{:S(2)}, u32[]{:S(2)}) async-start(f16[4,256,512]{2,1,0:T(8,128)(2,1)} %bitcast.80), calls=%async_computation.3 | async-start | bytes 2097152 | tf_op jit(solution)/shard_map/all_to_all | solution.py:31
  123.5 0.0 all-gather.3.cloned.1.call-start
  123.6 1.3 shard_map.88
  124.9 0.0 all-gather.3.cloned.1.call-update
  124.9 0.6 shard_map.95
  125.5 0.2 fusion.2.refs_0_
  125.7 5.5 %collective-permute-start.11 = (bf16[256,512]{1,0:T(8,128)(2,1)S(1)}, bf16[256,512]{1,0:T(8,128)(2,1)S(1)}, u32[]{:S(2)}, u32[]{:S(2)}) collective-permute-start(bf16[256,512]{1,0:T(8,128)(2,1)S(1)} %fusion.2.refs_0_), channel_id=1, source_target_pairs={{0,4},{4,8},{8,12},{12,0},{1,5},{5,9},{9,13},{13,1},{2,6},{6,10},{... | collective-permute-start | bytes 786440 | tf_op jit(solution)/shard_map/ppermute | solution.py:40
  131.1 2.3 %collective-permute-start.12 = (bf16[256,512]{1,0:T(8,128)(2,1)S(1)}, bf16[256,512]{1,0:T(8,128)(2,1)S(1)}, u32[]{:S(2)}, u32[]{:S(2)}) collective-permute-start(bf16[256,512]{1,0:T(8,128)(2,1)S(1)} %fusion.2.refs_0_), channel_id=1, source_target_pairs={{0,8},{4,12},{8,0},{12,4},{1,9},{5,13},{9,1},{13,5},{2,10},{6,14},... | collective-permute-start | bytes 786440 | tf_op jit(solution)/shard_map/ppermute | solution.py:40
  133.4 3.9 %collective-permute-start.13 = (bf16[256,512]{1,0:T(8,128)(2,1)S(1)}, bf16[256,512]{1,0:T(8,128)(2,1)S(1)}, u32[]{:S(2)}, u32[]{:S(2)}) collective-permute-start(bf16[256,512]{1,0:T(8,128)(2,1)S(1)} %fusion.2.refs_0_), channel_id=1, source_target_pairs={{0,12},{4,0},{8,4},{12,8},{1,13},{5,1},{9,5},{13,9},{2,14},{6,2},{... | collective-permute-start | bytes 786440 | tf_op jit(solution)/shard_map/ppermute | solution.py:40
  137.4 5.0 %collective-permute-done.12.refs_2_ = bf16[256,512]{1,0:T(8,128)(2,1)S(1)} collective-permute-done((bf16[256,512]{1,0:T(8,128)(2,1)S(1)}, bf16[256,512]{1,0:T(8,128)(2,1)S(1)}, u32[]{:S(2)}, u32[]{:S(2)}) %collective-permute-start.12) | collective-permute-done | bytes 262176 | tf_op jit(solution)/shard_map/ppermute | solution.py:40
  142.3 1.8 collective-permute-done.13.refs_3_
  144.1 0.6 shard_map.96
  144.8 3.9 %multiply_convert_fusion = f16[512,1024]{0,1:T(8,128)(2,1)} fusion(bf16[1024,512]{1,0:T(8,128)(2,1)S(1)} %bitcast.74, bf16[1024,1024]{1,0:T(8,128)(2,1)} %bitcast.14), kind=kOutput, calls=%fused_computation | convolution fusion | flops 1074790400 | bytes 4194304 | tf_op jit(solution)/shard_map/dot_general | solution.py:170
  148.6 4.5 %all-to-all-start.4 = ((f16[4,256,512]{2,1,0:T(8,128)(2,1)}), f16[4,256,512]{2,1,0:T(8,128)(2,1)}, u32[]{:S(2)}, u32[]{:S(2)}) async-start(f16[4,256,512]{2,1,0:T(8,128)(2,1)} %bitcast.31), calls=%async_computation.5 | async-start | bytes 2097152 | tf_op jit(solution)/shard_map/all_to_all | solution.py:31
  153.2 0.1 bitcast_convert_fusion.refs_0_
  153.3 21.1 %all-gather.3.cloned.1.call-done = f32[32,8,1024]{2,1,0:T(8,128)} async-done(((f32[2,8,1024]{2,1,0:T(8,128)}), f32[32,8,1024]{2,1,0:T(8,128)}) %all-gather.3.cloned.1.call-update) | async-done | bytes 1048592 | tf_op jit(solution)/shard_map/all_gather | solution.py:197
  174.4 1.2 copy-done.2
  175.6 0.7 shard_map.89
  176.3 1.3 add_bitcast_fusion.1
  177.6 0.9 all-to-all-done.4
  178.5 1.3 add_bitcast_fusion
  179.8 1.1 fusion.1
  (29 shorter events, 0.2 us)
Async XLA Ops:
  7.2 1.6 copy-start
  10.3 5.8 %copy-start.1 = (bf16[1,256,1024]{2,1,0:T(8,128)(2,1)S(1)}, bf16[1,256,1024]{2,1,0:T(8,128)(2,1)}, u32[]{:S(2)}) copy-start(bf16[1,256,1024]{2,1,0:T(8,128)(2,1)} %param.8) | copy-start | bytes 1572868
  10.3 46.6 %all-to-all-start = ((bf16[4,256,1024]{2,1,0:T(8,128)(2,1)}), bf16[4,256,1024]{2,1,0:T(8,128)(2,1)}, u32[]{:S(2)}, u32[]{:S(2)}) async-start(bf16[4,256,1024]{2,1,0:T(8,128)(2,1)} %shard_map.85.refs_0_), calls=%async_computation.1 | async-start | bytes 4194304 | tf_op jit(solution)/shard_map/all_to_all | solution.py:31
  15.3 49.8 %reduce-scatter.2.cloned.1.call-start = ((), (), s32[]{:S(2)}) async-start(), calls=%async_computation.6 | async-start | bytes 589824 | tf_op jit(solution)/shard_map/reduce_scatter | solution.py:156
  16.7 25.0 %copy-start.3 = (f32[4,8,1024]{2,1,0:T(8,128)S(1)}, f32[4,8,1024]{2,1,0:T(8,128)}, u32[]{:S(2)}) copy-start(f32[4,8,1024]{2,1,0:T(8,128)} %refs_4_.1) | copy-start | bytes 393220
  16.7 9.7 %collective-permute-start = (bf16[8,2,8,1024]{3,2,1,0:T(8,128)(2,1)S(1)}, bf16[8,2,8,1024]{3,2,1,0:T(8,128)(2,1)S(1)}, u32[]{:S(2)}, u32[]{:S(2)}) collective-permute-start(bf16[8,2,8,1024]{3,2,1,0:T(8,128)(2,1)S(1)} %dynamic-slice_bitcast_fusion), channel_id=1, source_target_pairs={{0,16},{16,0},{1,17},{17,1},{2,18},{18,2},{3,19},{19,3},{4,20},{20... | collective-permute-start | bytes 786440 | tf_op jit(solution)/shard_map/ppermute | solution.py:155
  27.4 15.7 %collective-permute-start.2 = (bf16[256,512]{1,0:T(8,128)(2,1)S(1)}, bf16[256,512]{1,0:T(8,128)(2,1)S(1)}, u32[]{:S(2)}, u32[]{:S(2)}) collective-permute-start(bf16[256,512]{1,0:T(8,128)(2,1)S(1)} %get-tuple-element.10.refs_1_), channel_id=1, source_target_pairs={{0,1},{1,2},{2,3},{3,0},{4,5},{5,6},{6,7},{7,4},{8,9},{9,10},{10,1... | collective-permute-start | bytes 786440 | tf_op jit(solution)/shard_map/ppermute | solution.py:40
  29.3 17.2 %collective-permute-start.3 = (bf16[256,512]{1,0:T(8,128)(2,1)S(1)}, bf16[256,512]{1,0:T(8,128)(2,1)S(1)}, u32[]{:S(2)}, u32[]{:S(2)}) collective-permute-start(bf16[256,512]{1,0:T(8,128)(2,1)S(1)} %get-tuple-element.9.refs_1_), channel_id=1, source_target_pairs={{0,1},{1,2},{2,3},{3,0},{4,5},{5,6},{6,7},{7,4},{8,9},{9,10},{10,1... | collective-permute-start | bytes 786440 | tf_op jit(solution)/shard_map/ppermute | solution.py:40
  31.2 25.1 %collective-permute-start.4 = (bf16[256,512]{1,0:T(8,128)(2,1)S(1)}, bf16[256,512]{1,0:T(8,128)(2,1)S(1)}, u32[]{:S(2)}, u32[]{:S(2)}) collective-permute-start(bf16[256,512]{1,0:T(8,128)(2,1)S(1)} %get-tuple-element.9.refs_1_), channel_id=1, source_target_pairs={{0,2},{1,3},{2,0},{3,1},{4,6},{5,7},{6,4},{7,5},{8,10},{9,11},{10,... | collective-permute-start | bytes 786440 | tf_op jit(solution)/shard_map/ppermute | solution.py:40
  36.7 19.6 %collective-permute-start.5 = (bf16[256,512]{1,0:T(8,128)(2,1)S(1)}, bf16[256,512]{1,0:T(8,128)(2,1)S(1)}, u32[]{:S(2)}, u32[]{:S(2)}) collective-permute-start(bf16[256,512]{1,0:T(8,128)(2,1)S(1)} %get-tuple-element.9.refs_1_), channel_id=1, source_target_pairs={{0,3},{1,0},{2,1},{3,2},{4,7},{5,4},{6,5},{7,6},{8,11},{9,8},{10,9... | collective-permute-start | bytes 786440 | tf_op jit(solution)/shard_map/ppermute | solution.py:40
  38.6 28.6 %collective-permute-start.10 = (bf16[256,512]{1,0:T(8,128)(2,1)S(1)}, bf16[256,512]{1,0:T(8,128)(2,1)S(1)}, u32[]{:S(2)}, u32[]{:S(2)}) collective-permute-start(bf16[256,512]{1,0:T(8,128)(2,1)S(1)} %get-tuple-element.10.refs_1_), channel_id=1, source_target_pairs={{0,3},{1,0},{2,1},{3,2},{4,7},{5,4},{6,5},{7,6},{8,11},{9,8},{10,9... | collective-permute-start | bytes 786440 | tf_op jit(solution)/shard_map/ppermute | solution.py:40
  43.1 35.7 %collective-permute-start.9 = (bf16[256,512]{1,0:T(8,128)(2,1)S(1)}, bf16[256,512]{1,0:T(8,128)(2,1)}, u32[]{:S(2)}, u32[]{:S(2)}) collective-permute-start(bf16[256,512]{1,0:T(8,128)(2,1)S(1)} %get-tuple-element.10.refs_1_), channel_id=1, source_target_pairs={{0,2},{1,3},{2,0},{3,1},{4,6},{5,7},{6,4},{7,5},{8,10},{9,11},{10,... | collective-permute-start | bytes 786440 | tf_op jit(solution)/shard_map/ppermute | solution.py:40
  60.8 22.9 %all-to-all-start.1 = ((f16[4,256,512]{2,1,0:T(8,128)(2,1)}), f16[4,256,512]{2,1,0:T(8,128)(2,1)S(1)}, u32[]{:S(2)}, u32[]{:S(2)}) async-start(f16[4,256,512]{2,1,0:T(8,128)(2,1)} %bitcast.78), calls=%async_computation.2 | async-start | bytes 2097152 | tf_op jit(solution)/shard_map/all_to_all | solution.py:31
  65.1 0.8 copy-start.5
  83.7 17.1 %copy-start.7 = (f32[1,8,1024]{2,1,0:T(8,128)S(1)}, f32[1,8,1024]{2,1,0:T(8,128)}, u32[]{:S(2)}) copy-start(f32[1,8,1024]{2,1,0:T(8,128)} %get-tuple-element.13) | copy-start | bytes 98308
  83.7 17.1 %copy-start.8 = (f32[1,8,1024]{2,1,0:T(8,128)S(1)}, f32[1,8,1024]{2,1,0:T(8,128)}, u32[]{:S(2)}) copy-start(f32[1,8,1024]{2,1,0:T(8,128)} %get-tuple-element.14) | copy-start | bytes 98308
  83.7 35.4 %all-to-all-start.3 = ((f16[4,256,512]{2,1,0:T(8,128)(2,1)}), f16[4,256,512]{2,1,0:T(8,128)(2,1)S(1)}, u32[]{:S(2)}, u32[]{:S(2)}) async-start(f16[4,256,512]{2,1,0:T(8,128)(2,1)} %bitcast.81), calls=%async_computation.4 | async-start | bytes 2097152 | tf_op jit(solution)/shard_map/all_to_all | solution.py:31
  90.0 18.0 %collective-permute-start.6 = (bf16[256,512]{1,0:T(8,128)(2,1)S(1)}, bf16[256,512]{1,0:T(8,128)(2,1)S(1)}, u32[]{:S(2)}, u32[]{:S(2)}) collective-permute-start(bf16[256,512]{1,0:T(8,128)(2,1)S(1)} %shard_map.91.refs_0_), channel_id=1, source_target_pairs={{0,4},{4,8},{8,12},{12,0},{1,5},{5,9},{9,13},{13,1},{2,6},{6,10},{... | collective-permute-start | bytes 786440 | tf_op jit(solution)/shard_map/ppermute | solution.py:40
  93.4 20.6 %collective-permute-start.7 = (bf16[256,512]{1,0:T(8,128)(2,1)S(1)}, bf16[256,512]{1,0:T(8,128)(2,1)S(1)}, u32[]{:S(2)}, u32[]{:S(2)}) collective-permute-start(bf16[256,512]{1,0:T(8,128)(2,1)S(1)} %shard_map.91.refs_0_), channel_id=1, source_target_pairs={{0,8},{4,12},{8,0},{12,4},{1,9},{5,13},{9,1},{13,5},{2,10},{6,14},... | collective-permute-start | bytes 786440 | tf_op jit(solution)/shard_map/ppermute | solution.py:40
  97.7 16.3 %collective-permute-start.8 = (bf16[256,512]{1,0:T(8,128)(2,1)S(1)}, bf16[256,512]{1,0:T(8,128)(2,1)S(1)}, u32[]{:S(2)}, u32[]{:S(2)}) collective-permute-start(bf16[256,512]{1,0:T(8,128)(2,1)S(1)} %shard_map.91.refs_0_), channel_id=1, source_target_pairs={{0,12},{4,0},{8,4},{12,8},{1,13},{5,1},{9,5},{13,9},{2,14},{6,2},{... | collective-permute-start | bytes 786440 | tf_op jit(solution)/shard_map/ppermute | solution.py:40
  100.8 13.7 %collective-permute-start.1 = (f32[4,8,1024]{2,1,0:T(8,128)S(1)}, f32[4,8,1024]{2,1,0:T(8,128)S(1)}, u32[]{:S(2)}, u32[]{:S(2)}) collective-permute-start(f32[4,8,1024]{2,1,0:T(8,128)S(1)} %pad_maximum_fusion.refs_1_), channel_id=1, source_target_pairs={{0,32},{32,0},{1,33},{33,1},{2,34},{34,2},{3,35},{35,3},{4,36},{36... | collective-permute-start | bytes 393224 | tf_op jit(solution)/shard_map/ppermute | solution.py:191
  119.1 4.5 %copy-start.6 = (bf16[1,256,1024]{2,1,0:T(8,128)(2,1)S(1)}, bf16[1,256,1024]{2,1,0:T(8,128)(2,1)}, u32[]{:S(2)}) copy-start(bf16[1,256,1024]{2,1,0:T(8,128)(2,1)} %param.7) | copy-start | bytes 1572868
  119.1 4.5 %copy-start.4 = (f32[4,8,1024]{2,1,0:T(8,128)S(1)}, f32[4,8,1024]{2,1,0:T(8,128)}, u32[]{:S(2)}) copy-start(f32[4,8,1024]{2,1,0:T(8,128)} %refs_3_.1) | copy-start | bytes 393220
  119.1 29.5 %all-to-all-start.2 = ((f16[4,256,512]{2,1,0:T(8,128)(2,1)}), f16[4,256,512]{2,1,0:T(8,128)(2,1)}, u32[]{:S(2)}, u32[]{:S(2)}) async-start(f16[4,256,512]{2,1,0:T(8,128)(2,1)} %bitcast.80), calls=%async_computation.3 | async-start | bytes 2097152 | tf_op jit(solution)/shard_map/all_to_all | solution.py:31
  123.5 50.9 %all-gather.3.cloned.1.call-start = ((), (), s32[]{:S(2)}) async-start(), calls=%async_computation.7 | async-start | bytes 1114112 | tf_op jit(solution)/shard_map/all_gather | solution.py:197
  125.7 11.7 %collective-permute-start.11 = (bf16[256,512]{1,0:T(8,128)(2,1)S(1)}, bf16[256,512]{1,0:T(8,128)(2,1)S(1)}, u32[]{:S(2)}, u32[]{:S(2)}) collective-permute-start(bf16[256,512]{1,0:T(8,128)(2,1)S(1)} %fusion.2.refs_0_), channel_id=1, source_target_pairs={{0,4},{4,8},{8,12},{12,0},{1,5},{5,9},{9,13},{13,1},{2,6},{6,10},{... | collective-permute-start | bytes 786440 | tf_op jit(solution)/shard_map/ppermute | solution.py:40
  131.1 11.2 %collective-permute-start.12 = (bf16[256,512]{1,0:T(8,128)(2,1)S(1)}, bf16[256,512]{1,0:T(8,128)(2,1)S(1)}, u32[]{:S(2)}, u32[]{:S(2)}) collective-permute-start(bf16[256,512]{1,0:T(8,128)(2,1)S(1)} %fusion.2.refs_0_), channel_id=1, source_target_pairs={{0,8},{4,12},{8,0},{12,4},{1,9},{5,13},{9,1},{13,5},{2,10},{6,14},... | collective-permute-start | bytes 786440 | tf_op jit(solution)/shard_map/ppermute | solution.py:40
  133.4 10.7 %collective-permute-start.13 = (bf16[256,512]{1,0:T(8,128)(2,1)S(1)}, bf16[256,512]{1,0:T(8,128)(2,1)S(1)}, u32[]{:S(2)}, u32[]{:S(2)}) collective-permute-start(bf16[256,512]{1,0:T(8,128)(2,1)S(1)} %fusion.2.refs_0_), channel_id=1, source_target_pairs={{0,12},{4,0},{8,4},{12,8},{1,13},{5,1},{9,5},{13,9},{2,14},{6,2},{... | collective-permute-start | bytes 786440 | tf_op jit(solution)/shard_map/ppermute | solution.py:40
  148.6 29.9 %all-to-all-start.4 = ((f16[4,256,512]{2,1,0:T(8,128)(2,1)}), f16[4,256,512]{2,1,0:T(8,128)(2,1)}, u32[]{:S(2)}, u32[]{:S(2)}) async-start(f16[4,256,512]{2,1,0:T(8,128)(2,1)} %bitcast.31), calls=%async_computation.5 | async-start | bytes 2097152 | tf_op jit(solution)/shard_map/all_to_all | solution.py:31
  174.4 1.2 copy-start.2
Sparse Core Ops, SparseCore 0:
  27.4 35.8 reduce-scatter.1
  126.7 47.6 all-gather.2

commit v4 on v3

--- a/solution.py
+++ b/solution.py
@@ -41,9 +41,14 @@
 
 
 def order_body(n, axis, at_ref, *refs):
-    pieces, out = refs[:n], refs[n]
-    for t in range(n):
-        out[lax.rem(at_ref[axis] + (n - t), n)] = pieces[t][...]
+    pieces, out, done = refs[:n], refs[n], refs[n + 1]
+    copies = [
+        pltpu.make_async_copy(pieces[t], out.at[lax.rem(at_ref[axis] + (n - t), n)], done.at[t]) for t in range(n)
+    ]
+    for copy in copies:
+        copy.start()
+    for copy in copies:
+        copy.wait()
 
 
 def copy_body(at_ref, in_ref, out_ref):
@@ -129,9 +134,19 @@
 
     def in_order(pieces, axis, after=()):
         shape = (n,) + pieces[0].shape
-        out = jax.ShapeDtypeStruct(shape, pieces[0].dtype)
-        body = functools.partial(order_body, n, axis)
-        return on_vmem(body, out, 0, 1 << 21, at, *pieces, after=after).reshape(n * shape[1], shape[2])
+        skip = len(after)
+
+        def called(at_ref, *refs):
+            order_body(n, axis, at_ref, *refs[skip:])
+
+        return pl.pallas_call(
+            called,
+            out_shape=jax.ShapeDtypeStruct(shape, pieces[0].dtype),
+            in_specs=[SMEM] + [ANY] * (skip + n),
+            out_specs=VMEM,
+            scratch_shapes=[pltpu.SemaphoreType.DMA((n,))],
+            compiler_params=pltpu.CompilerParams(vmem_limit_bytes=VMEM_LIMIT),
+        )(at, *after, *pieces).reshape(n * shape[1], shape[2])
 
     blocks = pl.pallas_call(
         functools.partial(split_body, n),
@@ -177,10 +192,8 @@
         aims = wanted[:, c] if k == 0 else hold(wanted[:, c], [residual])
         shares = project(k)
         if k < last:
-            weights.append(in_order(pieces[k + 1], 1, after=[shares[0, :8, :128].astype(jnp.float32)]))
+            weights.append(in_order(pieces[k + 1], 1, after=[shares[0, :8, :128].astype(jnp.float32), part]))
         residual = residual_of(exchange(shares, "x"), aims)
-        if k == 0:
-            residual = hold(residual, [part])
         whole.append(in_order([residual] + [shift(residual, "x", s) for s in range(1, n)], 0))
 
     g_piece = lax.dynamic_index_in_dim(outer_params, which, 0, keepdims=False)

time: 192 us -> 191 us (level)
  the two profiles are of different devices: /device:TPU:1 before, /device:TPU:2 now
where the time goes in v4:
time: 191 us; the launch traced here: 190 us
  starting transfers between devices  75.1 us (39%)
  waiting for transfers between devices  62.9 us (33%)
  matrix products  15.4 us (8%)
  between operations  15.1 us (8%)
  Pallas kernels  9.38 us (5%)
  other arithmetic  6.87 us (4%)
  local copies, waits for them, and re-layouts  5.16 us (3%)
    ppermute x12, starting transfers between devices, shift(): return lax.ppermute(block, axis, [(k, (k + s) % n) for k in range(n)])  39 us
    ppermute x12, waiting for transfers between devices, shift(): return lax.ppermute(block, axis, [(k, (k + s) % n) for k in range(n)])  37.4 us
    all_to_all x5, starting transfers between devices, exchange(): return lax.all_to_all(blocks, axis, 0, 0, tiled=True)  31.7 us
    all_gather x1, waiting for transfers between devices, on_device(): lax.all_gather(pair, ('z', 'core'), axis=0, tiled=False)  17.3 us
    dot_general x2, matrix products, gradient(): lax.dot_general(block, rowwise(res.reshape(n * count, -1)), (((0,), (0,))...  7.79 us
    dot_general x2, matrix products, project(): shares = jnp.dot(block, weights[k], preferred_element_type=jnp.float32)  7.64 us
    all_to_all x5, waiting for transfers between devices, exchange(): return lax.all_to_all(blocks, axis, 0, 0, tiled=True)  5.06 us
    pallas_call x6, Pallas kernels, on_vmem(): pl.pallas_call(called, out_shape=outs, in_specs=[SMEM] + [ANY] * skip + [...  4.23 us
  transfers between devices with their start and end apart: 21, of which 13 were waited for; matrix products, arithmetic and copies ran while one was open for 11% of the time, Pallas kernels for 4%

profile of v4, /device:TPU:2, one launch (start us, length us, event | category | flops | bytes accessed | tf_op | source)
XLA Modules:
  0.0 189.9 jit_solution(14451308295128982356)
XLA Ops:
  7.2 1.6 copy-done
  8.8 1.6 shard_map.85.refs_0_
  10.3 0.0 copy-start.1
  10.3 10.5 %all-to-all-start = ((bf16[4,256,1024]{2,1,0:T(8,128)(2,1)}), bf16[4,256,1024]{2,1,0:T(8,128)(2,1)}, u32[]{:S(2)}, u32[]{:S(2)}) async-start(bf16[4,256,1024]{2,1,0:T(8,128)(2,1)} %shard_map.85.refs_0_), calls=%async_computation.1 | async-start | bytes 4194304 | tf_op jit(solution)/shard_map/all_to_all | solution.py:31
  21.5 0.1 pad_add_fusion.at_ref
  21.6 0.6 shard_map.86
  22.1 0.0 copy-start.3
  22.2 2.1 %collective-permute-start = (bf16[8,2,8,1024]{3,2,1,0:T(8,128)(2,1)S(1)}, bf16[8,2,8,1024]{3,2,1,0:T(8,128)(2,1)S(1)}, u32[]{:S(2)}, u32[]{:S(2)}) collective-permute-start(bf16[8,2,8,1024]{3,2,1,0:T(8,128)(2,1)S(1)} %dynamic-slice_bitcast_fusion), channel_id=1, source_target_pairs={{0,16},{16,0},{1,17},{17,1},{2,18},{18,2},{3,19},{19,3},{4,20},{20... | collective-permute-start | bytes 786440 | tf_op jit(solution)/shard_map/ppermute | solution.py:170
  24.3 1.5 collective-permute-done
  25.8 0.9 convert_add_fusion
  26.6 0.0 reduce-scatter.2.cloned.1.call-update
  26.7 1.9 %collective-permute-start.2 = (bf16[256,512]{1,0:T(8,128)(2,1)S(1)}, bf16[256,512]{1,0:T(8,128)(2,1)S(1)}, u32[]{:S(2)}, u32[]{:S(2)}) collective-permute-start(bf16[256,512]{1,0:T(8,128)(2,1)S(1)} %get-tuple-element.10.refs_2_), channel_id=1, source_target_pairs={{0,1},{1,2},{2,3},{3,0},{4,5},{5,6},{6,7},{7,4},{8,9},{9,10},{10,1... | collective-permute-start | bytes 786440 | tf_op jit(solution)/shard_map/ppermute | solution.py:40
  28.6 1.9 %collective-permute-start.3 = (bf16[256,512]{1,0:T(8,128)(2,1)S(1)}, bf16[256,512]{1,0:T(8,128)(2,1)S(1)}, u32[]{:S(2)}, u32[]{:S(2)}) collective-permute-start(bf16[256,512]{1,0:T(8,128)(2,1)S(1)} %get-tuple-element.9.refs_1_), channel_id=1, source_target_pairs={{0,1},{1,2},{2,3},{3,0},{4,5},{5,6},{6,7},{7,4},{8,9},{9,10},{10,1... | collective-permute-start | bytes 786440 | tf_op jit(solution)/shard_map/ppermute | solution.py:40
  30.5 6.3 %collective-permute-start.4 = (bf16[256,512]{1,0:T(8,128)(2,1)S(1)}, bf16[256,512]{1,0:T(8,128)(2,1)S(1)}, u32[]{:S(2)}, u32[]{:S(2)}) collective-permute-start(bf16[256,512]{1,0:T(8,128)(2,1)S(1)} %get-tuple-element.9.refs_1_), channel_id=1, source_target_pairs={{0,2},{1,3},{2,0},{3,1},{4,6},{5,7},{6,4},{7,5},{8,10},{9,11},{10,... | collective-permute-start | bytes 786440 | tf_op jit(solution)/shard_map/ppermute | solution.py:40
  36.8 1.9 %collective-permute-start.5 = (bf16[256,512]{1,0:T(8,128)(2,1)S(1)}, bf16[256,512]{1,0:T(8,128)(2,1)S(1)}, u32[]{:S(2)}, u32[]{:S(2)}) collective-permute-start(bf16[256,512]{1,0:T(8,128)(2,1)S(1)} %get-tuple-element.9.refs_1_), channel_id=1, source_target_pairs={{0,3},{1,0},{2,1},{3,2},{4,7},{5,4},{6,5},{7,6},{8,11},{9,8},{10,9... | collective-permute-start | bytes 786440 | tf_op jit(solution)/shard_map/ppermute | solution.py:40
  38.7 3.4 %collective-permute-start.10 = (bf16[256,512]{1,0:T(8,128)(2,1)S(1)}, bf16[256,512]{1,0:T(8,128)(2,1)S(1)}, u32[]{:S(2)}, u32[]{:S(2)}) collective-permute-start(bf16[256,512]{1,0:T(8,128)(2,1)S(1)} %get-tuple-element.10.refs_2_), channel_id=1, source_target_pairs={{0,3},{1,0},{2,1},{3,2},{4,7},{5,4},{6,5},{7,6},{8,11},{9,8},{10,9... | collective-permute-start | bytes 786440 | tf_op jit(solution)/shard_map/ppermute | solution.py:40
  42.1 1.4 constant_dynamic-slice_fusion
  43.5 3.9 %collective-permute-start.9 = (bf16[256,512]{1,0:T(8,128)(2,1)S(1)}, bf16[256,512]{1,0:T(8,128)(2,1)}, u32[]{:S(2)}, u32[]{:S(2)}) collective-permute-start(bf16[256,512]{1,0:T(8,128)(2,1)S(1)} %get-tuple-element.10.refs_2_), channel_id=1, source_target_pairs={{0,2},{1,3},{2,0},{3,1},{4,6},{5,7},{6,4},{7,5},{8,10},{9,11},{10,... | collective-permute-start | bytes 786440 | tf_op jit(solution)/shard_map/ppermute | solution.py:40
  47.5 8.3 %collective-permute-done.4.refs_3_ = bf16[256,512]{1,0:T(8,128)(2,1)S(1)} collective-permute-done((bf16[256,512]{1,0:T(8,128)(2,1)S(1)}, bf16[256,512]{1,0:T(8,128)(2,1)S(1)}, u32[]{:S(2)}, u32[]{:S(2)}) %collective-permute-start.4) | collective-permute-done | bytes 262176 | tf_op jit(solution)/shard_map/ppermute | solution.py:40
  55.8 0.7 shard_map.90
  56.4 3.8 %multiply_convert_fusion.3 = f16[512,1024]{0,1:T(8,128)(2,1)} fusion(bf16[1024,1024]{1,0:T(8,128)(2,1)} %bitcast.14, bf16[1024,512]{1,0:T(8,128)(2,1)S(1)} %bitcast.72), kind=kOutput, calls=%fused_computation.3 | convolution fusion | flops 1074790400 | bytes 4194304 | tf_op jit(solution)/shard_map/dot_general | solution.py:176
  60.3 4.8 %all-to-all-start.1 = ((f16[4,256,512]{2,1,0:T(8,128)(2,1)}), f16[4,256,512]{2,1,0:T(8,128)(2,1)S(1)}, u32[]{:S(2)}, u32[]{:S(2)}) async-start(f16[4,256,512]{2,1,0:T(8,128)(2,1)} %bitcast.78), calls=%async_computation.2 | async-start | bytes 2097152 | tf_op jit(solution)/shard_map/all_to_all | solution.py:31
  65.1 1.6 reduce-scatter.2.cloned.1.call-done
  66.7 0.8 copy-done.5
  67.6 0.5 shard_map.87.refs_1_
  68.1 0.7 fusion.4.refs_0_
  68.8 9.4 %collective-permute-done.9.refs_4_ = bf16[256,512]{1,0:T(8,128)(2,1)} collective-permute-done((bf16[256,512]{1,0:T(8,128)(2,1)S(1)}, bf16[256,512]{1,0:T(8,128)(2,1)}, u32[]{:S(2)}, u32[]{:S(2)}) %collective-permute-start.9) | collective-permute-done | bytes 262176 | tf_op jit(solution)/shard_map/ppermute | solution.py:40
  78.2 1.6 shard_map.93
  79.8 3.8 %multiply_convert_fusion.1 = f16[512,1024]{0,1:T(8,128)(2,1)} fusion(bf16[1024,1024]{1,0:T(8,128)(2,1)} %bitcast.14, bf16[1024,512]{1,0:T(8,128)(2,1)S(1)} %bitcast.73), kind=kOutput, calls=%fused_computation.1 | convolution fusion | flops 1074790400 | bytes 4194304 | tf_op jit(solution)/shard_map/dot_general | solution.py:176
  83.6 4.9 %all-to-all-start.3 = ((f16[4,256,512]{2,1,0:T(8,128)(2,1)}), f16[4,256,512]{2,1,0:T(8,128)(2,1)S(1)}, u32[]{:S(2)}, u32[]{:S(2)}) async-start(f16[4,256,512]{2,1,0:T(8,128)(2,1)} %bitcast.81), calls=%async_computation.4 | async-start | bytes 2097152 | tf_op jit(solution)/shard_map/all_to_all | solution.py:31
  88.6 1.2 fusion.3.refs_0_
  89.8 3.4 %collective-permute-start.6 = (bf16[256,512]{1,0:T(8,128)(2,1)S(1)}, bf16[256,512]{1,0:T(8,128)(2,1)S(1)}, u32[]{:S(2)}, u32[]{:S(2)}) collective-permute-start(bf16[256,512]{1,0:T(8,128)(2,1)S(1)} %fusion.3.refs_0_), channel_id=1, source_target_pairs={{0,4},{4,8},{8,12},{12,0},{1,5},{5,9},{9,13},{13,1},{2,6},{6,10},{... | collective-permute-start | bytes 786440 | tf_op jit(solution)/shard_map/ppermute | solution.py:40
  93.1 2.5 %collective-permute-start.7 = (bf16[256,512]{1,0:T(8,128)(2,1)S(1)}, bf16[256,512]{1,0:T(8,128)(2,1)S(1)}, u32[]{:S(2)}, u32[]{:S(2)}) collective-permute-start(bf16[256,512]{1,0:T(8,128)(2,1)S(1)} %fusion.3.refs_0_), channel_id=1, source_target_pairs={{0,8},{4,12},{8,0},{12,4},{1,9},{5,13},{9,1},{13,5},{2,10},{6,14},... | collective-permute-start | bytes 786440 | tf_op jit(solution)/shard_map/ppermute | solution.py:40
  95.7 4.5 %collective-permute-start.8 = (bf16[256,512]{1,0:T(8,128)(2,1)S(1)}, bf16[256,512]{1,0:T(8,128)(2,1)S(1)}, u32[]{:S(2)}, u32[]{:S(2)}) collective-permute-start(bf16[256,512]{1,0:T(8,128)(2,1)S(1)} %fusion.3.refs_0_), channel_id=1, source_target_pairs={{0,12},{4,0},{8,4},{12,8},{1,13},{5,1},{9,5},{13,9},{2,14},{6,2},{... | collective-permute-start | bytes 786440 | tf_op jit(solution)/shard_map/ppermute | solution.py:40
  100.3 2.4 %collective-permute-start.1 = (f32[4,8,1024]{2,1,0:T(8,128)S(1)}, f32[4,8,1024]{2,1,0:T(8,128)S(1)}, u32[]{:S(2)}, u32[]{:S(2)}) collective-permute-start(f32[4,8,1024]{2,1,0:T(8,128)S(1)} %pad_maximum_fusion.refs_1_), channel_id=1, source_target_pairs={{0,32},{32,0},{1,33},{33,1},{2,34},{34,2},{3,35},{35,3},{4,36},{36... | collective-permute-start | bytes 393224 | tf_op jit(solution)/shard_map/ppermute | solution.py:204
  102.7 4.6 %collective-permute-done.6.refs_1_ = bf16[256,512]{1,0:T(8,128)(2,1)S(1)} collective-permute-done((bf16[256,512]{1,0:T(8,128)(2,1)S(1)}, bf16[256,512]{1,0:T(8,128)(2,1)S(1)}, u32[]{:S(2)}, u32[]{:S(2)}) %collective-permute-start.6) | collective-permute-done | bytes 262176 | tf_op jit(solution)/shard_map/ppermute | solution.py:40
  107.2 2.1 %collective-permute-done.7.refs_2_ = bf16[256,512]{1,0:T(8,128)(2,1)S(1)} collective-permute-done((bf16[256,512]{1,0:T(8,128)(2,1)S(1)}, bf16[256,512]{1,0:T(8,128)(2,1)S(1)}, u32[]{:S(2)}, u32[]{:S(2)}) %collective-permute-start.7) | collective-permute-done | bytes 262176 | tf_op jit(solution)/shard_map/ppermute | solution.py:40
  109.3 4.3 %collective-permute-done.8.refs_3_ = bf16[256,512]{1,0:T(8,128)(2,1)S(1)} collective-permute-done((bf16[256,512]{1,0:T(8,128)(2,1)S(1)}, bf16[256,512]{1,0:T(8,128)(2,1)S(1)}, u32[]{:S(2)}, u32[]{:S(2)}) %collective-permute-start.8) | collective-permute-done | bytes 262176 | tf_op jit(solution)/shard_map/ppermute | solution.py:40
  113.6 0.7 shard_map.91
  114.3 0.6 shard_map.92
  114.9 3.9 %multiply_convert_fusion.2 = f16[512,1024]{0,1:T(8,128)(2,1)} fusion(bf16[1024,512]{1,0:T(8,128)(2,1)S(1)} %shard_map.92, bf16[1024,1024]{1,0:T(8,128)(2,1)} %bitcast.14), kind=kOutput, calls=%fused_computation.2 | convolution fusion | flops 1074790400 | bytes 4194304 | tf_op jit(solution)/shard_map/dot_general | solution.py:185
  118.9 7.1 %all-to-all-start.2 = ((f16[4,256,512]{2,1,0:T(8,128)(2,1)}), f16[4,256,512]{2,1,0:T(8,128)(2,1)}, u32[]{:S(2)}, u32[]{:S(2)}) async-start(f16[4,256,512]{2,1,0:T(8,128)(2,1)} %bitcast.80), calls=%async_computation.3 | async-start | bytes 2097152 | tf_op jit(solution)/shard_map/all_to_all | solution.py:31
  126.0 1.3 shard_map.88
  127.3 0.0 all-gather.3.cloned.1.call-update
  127.3 0.6 shard_map.94
  127.9 0.2 fusion.2.refs_0_
  128.1 1.9 %collective-permute-start.11 = (bf16[256,512]{1,0:T(8,128)(2,1)S(1)}, bf16[256,512]{1,0:T(8,128)(2,1)S(1)}, u32[]{:S(2)}, u32[]{:S(2)}) collective-permute-start(bf16[256,512]{1,0:T(8,128)(2,1)S(1)} %fusion.2.refs_0_), channel_id=1, source_target_pairs={{0,4},{4,8},{8,12},{12,0},{1,5},{5,9},{9,13},{13,1},{2,6},{6,10},{... | collective-permute-start | bytes 786440 | tf_op jit(solution)/shard_map/ppermute | solution.py:40
  130.0 5.4 %collective-permute-start.12 = (bf16[256,512]{1,0:T(8,128)(2,1)S(1)}, bf16[256,512]{1,0:T(8,128)(2,1)S(1)}, u32[]{:S(2)}, u32[]{:S(2)}) collective-permute-start(bf16[256,512]{1,0:T(8,128)(2,1)S(1)} %fusion.2.refs_0_), channel_id=1, source_target_pairs={{0,8},{4,12},{8,0},{12,4},{1,9},{5,13},{9,1},{13,5},{2,10},{6,14},... | collective-permute-start | bytes 786440 | tf_op jit(solution)/shard_map/ppermute | solution.py:40
  135.4 1.9 %collective-permute-start.13 = (bf16[256,512]{1,0:T(8,128)(2,1)S(1)}, bf16[256,512]{1,0:T(8,128)(2,1)S(1)}, u32[]{:S(2)}, u32[]{:S(2)}) collective-permute-start(bf16[256,512]{1,0:T(8,128)(2,1)S(1)} %fusion.2.refs_0_), channel_id=1, source_target_pairs={{0,12},{4,0},{8,4},{12,8},{1,13},{5,1},{9,5},{13,9},{2,14},{6,2},{... | collective-permute-start | bytes 786440 | tf_op jit(solution)/shard_map/ppermute | solution.py:40
  137.4 1.8 collective-permute-done.11.refs_1_
  139.2 3.5 %collective-permute-done.12.refs_2_ = bf16[256,512]{1,0:T(8,128)(2,1)S(1)} collective-permute-done((bf16[256,512]{1,0:T(8,128)(2,1)S(1)}, bf16[256,512]{1,0:T(8,128)(2,1)S(1)}, u32[]{:S(2)}, u32[]{:S(2)}) %collective-permute-start.12) | collective-permute-done | bytes 262176 | tf_op jit(solution)/shard_map/ppermute | solution.py:40
  142.7 3.3 %collective-permute-done.13.refs_3_ = bf16[256,512]{1,0:T(8,128)(2,1)S(1)} collective-permute-done((bf16[256,512]{1,0:T(8,128)(2,1)S(1)}, bf16[256,512]{1,0:T(8,128)(2,1)S(1)}, u32[]{:S(2)}, u32[]{:S(2)}) %collective-permute-start.13) | collective-permute-done | bytes 262176 | tf_op jit(solution)/shard_map/ppermute | solution.py:40
  146.0 0.7 shard_map.95
  146.7 3.9 %multiply_convert_fusion = f16[512,1024]{0,1:T(8,128)(2,1)} fusion(bf16[1024,512]{1,0:T(8,128)(2,1)S(1)} %bitcast.74, bf16[1024,1024]{1,0:T(8,128)(2,1)} %bitcast.14), kind=kOutput, calls=%fused_computation | convolution fusion | flops 1074790400 | bytes 4194304 | tf_op jit(solution)/shard_map/dot_general | solution.py:185
  150.6 0.5 all-to-all-done.2
  151.1 4.4 %all-to-all-start.4 = ((f16[4,256,512]{2,1,0:T(8,128)(2,1)}), f16[4,256,512]{2,1,0:T(8,128)(2,1)}, u32[]{:S(2)}, u32[]{:S(2)}) async-start(f16[4,256,512]{2,1,0:T(8,128)(2,1)} %bitcast.31), calls=%async_computation.5 | async-start | bytes 2097152 | tf_op jit(solution)/shard_map/all_to_all | solution.py:31
  155.4 0.1 bitcast_convert_fusion.refs_0_
  155.5 17.3 %all-gather.3.cloned.1.call-done = f32[32,8,1024]{2,1,0:T(8,128)} async-done(((f32[2,8,1024]{2,1,0:T(8,128)}), f32[32,8,1024]{2,1,0:T(8,128)}) %all-gather.3.cloned.1.call-update) | async-done | bytes 1048592 | tf_op jit(solution)/shard_map/all_gather | solution.py:210
  172.8 1.2 copy-done.2
  174.0 0.7 shard_map.89
  174.7 1.3 add_bitcast_fusion.1
  176.0 4.6 %all-to-all-done.4 = f16[4,256,512]{2,1,0:T(8,128)(2,1)} async-done(((f16[4,256,512]{2,1,0:T(8,128)(2,1)}), f16[4,256,512]{2,1,0:T(8,128)(2,1)}, u32[]{:S(2)}, u32[]{:S(2)}) %all-to-all-start.4) | async-done | bytes 1048608 | tf_op jit(solution)/shard_map/all_to_all | solution.py:31
  180.6 1.3 add_bitcast_fusion
  181.9 1.1 fusion.1
  (28 shorter events, 0.2 us)
Async XLA Ops:
  7.2 1.6 copy-start
  10.3 11.2 %copy-start.1 = (bf16[1,256,1024]{2,1,0:T(8,128)(2,1)S(1)}, bf16[1,256,1024]{2,1,0:T(8,128)(2,1)}, u32[]{:S(2)}) copy-start(bf16[1,256,1024]{2,1,0:T(8,128)(2,1)} %param.8) | copy-start | bytes 1572868
  10.3 46.1 %all-to-all-start = ((bf16[4,256,1024]{2,1,0:T(8,128)(2,1)}), bf16[4,256,1024]{2,1,0:T(8,128)(2,1)}, u32[]{:S(2)}, u32[]{:S(2)}) async-start(bf16[4,256,1024]{2,1,0:T(8,128)(2,1)} %shard_map.85.refs_0_), calls=%async_computation.1 | async-start | bytes 4194304 | tf_op jit(solution)/shard_map/all_to_all | solution.py:31
  20.8 45.9 %reduce-scatter.2.cloned.1.call-start = ((), (), s32[]{:S(2)}) async-start(), calls=%async_computation.6 | async-start | bytes 589824 | tf_op jit(solution)/shard_map/reduce_scatter | solution.py:171
  22.1 20.0 %copy-start.3 = (f32[4,8,1024]{2,1,0:T(8,128)S(1)}, f32[4,8,1024]{2,1,0:T(8,128)}, u32[]{:S(2)}) copy-start(f32[4,8,1024]{2,1,0:T(8,128)} %refs_4_.1) | copy-start | bytes 393220
  22.2 3.6 %collective-permute-start = (bf16[8,2,8,1024]{3,2,1,0:T(8,128)(2,1)S(1)}, bf16[8,2,8,1024]{3,2,1,0:T(8,128)(2,1)S(1)}, u32[]{:S(2)}, u32[]{:S(2)}) collective-permute-start(bf16[8,2,8,1024]{3,2,1,0:T(8,128)(2,1)S(1)} %dynamic-slice_bitcast_fusion), channel_id=1, source_target_pairs={{0,16},{16,0},{1,17},{17,1},{2,18},{18,2},{3,19},{19,3},{4,20},{20... | collective-permute-start | bytes 786440 | tf_op jit(solution)/shard_map/ppermute | solution.py:170
  26.7 16.9 %collective-permute-start.2 = (bf16[256,512]{1,0:T(8,128)(2,1)S(1)}, bf16[256,512]{1,0:T(8,128)(2,1)S(1)}, u32[]{:S(2)}, u32[]{:S(2)}) collective-permute-start(bf16[256,512]{1,0:T(8,128)(2,1)S(1)} %get-tuple-element.10.refs_2_), channel_id=1, source_target_pairs={{0,1},{1,2},{2,3},{3,0},{4,5},{5,6},{6,7},{7,4},{8,9},{9,10},{10,1... | collective-permute-start | bytes 786440 | tf_op jit(solution)/shard_map/ppermute | solution.py:40
  28.6 18.9 %collective-permute-start.3 = (bf16[256,512]{1,0:T(8,128)(2,1)S(1)}, bf16[256,512]{1,0:T(8,128)(2,1)S(1)}, u32[]{:S(2)}, u32[]{:S(2)}) collective-permute-start(bf16[256,512]{1,0:T(8,128)(2,1)S(1)} %get-tuple-element.9.refs_1_), channel_id=1, source_target_pairs={{0,1},{1,2},{2,3},{3,0},{4,5},{5,6},{6,7},{7,4},{8,9},{9,10},{10,1... | collective-permute-start | bytes 786440 | tf_op jit(solution)/shard_map/ppermute | solution.py:40
  30.5 25.2 %collective-permute-start.4 = (bf16[256,512]{1,0:T(8,128)(2,1)S(1)}, bf16[256,512]{1,0:T(8,128)(2,1)S(1)}, u32[]{:S(2)}, u32[]{:S(2)}) collective-permute-start(bf16[256,512]{1,0:T(8,128)(2,1)S(1)} %get-tuple-element.9.refs_1_), channel_id=1, source_target_pairs={{0,2},{1,3},{2,0},{3,1},{4,6},{5,7},{6,4},{7,5},{8,10},{9,11},{10,... | collective-permute-start | bytes 786440 | tf_op jit(solution)/shard_map/ppermute | solution.py:40
  36.8 18.9 %collective-permute-start.5 = (bf16[256,512]{1,0:T(8,128)(2,1)S(1)}, bf16[256,512]{1,0:T(8,128)(2,1)S(1)}, u32[]{:S(2)}, u32[]{:S(2)}) collective-permute-start(bf16[256,512]{1,0:T(8,128)(2,1)S(1)} %get-tuple-element.9.refs_1_), channel_id=1, source_target_pairs={{0,3},{1,0},{2,1},{3,2},{4,7},{5,4},{6,5},{7,6},{8,11},{9,8},{10,9... | collective-permute-start | bytes 786440 | tf_op jit(solution)/shard_map/ppermute | solution.py:40
  38.7 30.0 %collective-permute-start.10 = (bf16[256,512]{1,0:T(8,128)(2,1)S(1)}, bf16[256,512]{1,0:T(8,128)(2,1)S(1)}, u32[]{:S(2)}, u32[]{:S(2)}) collective-permute-start(bf16[256,512]{1,0:T(8,128)(2,1)S(1)} %get-tuple-element.10.refs_2_), channel_id=1, source_target_pairs={{0,3},{1,0},{2,1},{3,2},{4,7},{5,4},{6,5},{7,6},{8,11},{9,8},{10,9... | collective-permute-start | bytes 786440 | tf_op jit(solution)/shard_map/ppermute | solution.py:40
  43.5 34.7 %collective-permute-start.9 = (bf16[256,512]{1,0:T(8,128)(2,1)S(1)}, bf16[256,512]{1,0:T(8,128)(2,1)}, u32[]{:S(2)}, u32[]{:S(2)}) collective-permute-start(bf16[256,512]{1,0:T(8,128)(2,1)S(1)} %get-tuple-element.10.refs_2_), channel_id=1, source_target_pairs={{0,2},{1,3},{2,0},{3,1},{4,6},{5,7},{6,4},{7,5},{8,10},{9,11},{10,... | collective-permute-start | bytes 786440 | tf_op jit(solution)/shard_map/ppermute | solution.py:40
  60.3 23.4 %all-to-all-start.1 = ((f16[4,256,512]{2,1,0:T(8,128)(2,1)}), f16[4,256,512]{2,1,0:T(8,128)(2,1)S(1)}, u32[]{:S(2)}, u32[]{:S(2)}) async-start(f16[4,256,512]{2,1,0:T(8,128)(2,1)} %bitcast.78), calls=%async_computation.2 | async-start | bytes 2097152 | tf_op jit(solution)/shard_map/all_to_all | solution.py:31
  66.7 0.8 copy-start.5
  83.6 16.6 %copy-start.7 = (f32[1,8,1024]{2,1,0:T(8,128)S(1)}, f32[1,8,1024]{2,1,0:T(8,128)}, u32[]{:S(2)}) copy-start(f32[1,8,1024]{2,1,0:T(8,128)} %get-tuple-element.13) | copy-start | bytes 98308
  83.6 16.6 %copy-start.8 = (f32[1,8,1024]{2,1,0:T(8,128)S(1)}, f32[1,8,1024]{2,1,0:T(8,128)}, u32[]{:S(2)}) copy-start(f32[1,8,1024]{2,1,0:T(8,128)} %get-tuple-element.14) | copy-start | bytes 98308
  83.6 35.2 %all-to-all-start.3 = ((f16[4,256,512]{2,1,0:T(8,128)(2,1)}), f16[4,256,512]{2,1,0:T(8,128)(2,1)S(1)}, u32[]{:S(2)}, u32[]{:S(2)}) async-start(f16[4,256,512]{2,1,0:T(8,128)(2,1)} %bitcast.81), calls=%async_computation.4 | async-start | bytes 2097152 | tf_op jit(solution)/shard_map/all_to_all | solution.py:31
  89.8 17.5 %collective-permute-start.6 = (bf16[256,512]{1,0:T(8,128)(2,1)S(1)}, bf16[256,512]{1,0:T(8,128)(2,1)S(1)}, u32[]{:S(2)}, u32[]{:S(2)}) collective-permute-start(bf16[256,512]{1,0:T(8,128)(2,1)S(1)} %fusion.3.refs_0_), channel_id=1, source_target_pairs={{0,4},{4,8},{8,12},{12,0},{1,5},{5,9},{9,13},{13,1},{2,6},{6,10},{... | collective-permute-start | bytes 786440 | tf_op jit(solution)/shard_map/ppermute | solution.py:40
  93.1 16.2 %collective-permute-start.7 = (bf16[256,512]{1,0:T(8,128)(2,1)S(1)}, bf16[256,512]{1,0:T(8,128)(2,1)S(1)}, u32[]{:S(2)}, u32[]{:S(2)}) collective-permute-start(bf16[256,512]{1,0:T(8,128)(2,1)S(1)} %fusion.3.refs_0_), channel_id=1, source_target_pairs={{0,8},{4,12},{8,0},{12,4},{1,9},{5,13},{9,1},{13,5},{2,10},{6,14},... | collective-permute-start | bytes 786440 | tf_op jit(solution)/shard_map/ppermute | solution.py:40
  95.7 18.0 %collective-permute-start.8 = (bf16[256,512]{1,0:T(8,128)(2,1)S(1)}, bf16[256,512]{1,0:T(8,128)(2,1)S(1)}, u32[]{:S(2)}, u32[]{:S(2)}) collective-permute-start(bf16[256,512]{1,0:T(8,128)(2,1)S(1)} %fusion.3.refs_0_), channel_id=1, source_target_pairs={{0,12},{4,0},{8,4},{12,8},{1,13},{5,1},{9,5},{13,9},{2,14},{6,2},{... | collective-permute-start | bytes 786440 | tf_op jit(solution)/shard_map/ppermute | solution.py:40
  100.3 14.1 %collective-permute-start.1 = (f32[4,8,1024]{2,1,0:T(8,128)S(1)}, f32[4,8,1024]{2,1,0:T(8,128)S(1)}, u32[]{:S(2)}, u32[]{:S(2)}) collective-permute-start(f32[4,8,1024]{2,1,0:T(8,128)S(1)} %pad_maximum_fusion.refs_1_), channel_id=1, source_target_pairs={{0,32},{32,0},{1,33},{33,1},{2,34},{34,2},{3,35},{35,3},{4,36},{36... | collective-permute-start | bytes 393224 | tf_op jit(solution)/shard_map/ppermute | solution.py:204
  118.9 7.1 %copy-start.6 = (bf16[1,256,1024]{2,1,0:T(8,128)(2,1)S(1)}, bf16[1,256,1024]{2,1,0:T(8,128)(2,1)}, u32[]{:S(2)}) copy-start(bf16[1,256,1024]{2,1,0:T(8,128)(2,1)} %param.7) | copy-start | bytes 1572868
  118.9 7.1 %copy-start.4 = (f32[4,8,1024]{2,1,0:T(8,128)S(1)}, f32[4,8,1024]{2,1,0:T(8,128)}, u32[]{:S(2)}) copy-start(f32[4,8,1024]{2,1,0:T(8,128)} %refs_3_.1) | copy-start | bytes 393220
  118.9 32.2 %all-to-all-start.2 = ((f16[4,256,512]{2,1,0:T(8,128)(2,1)}), f16[4,256,512]{2,1,0:T(8,128)(2,1)}, u32[]{:S(2)}, u32[]{:S(2)}) async-start(f16[4,256,512]{2,1,0:T(8,128)(2,1)} %bitcast.80), calls=%async_computation.3 | async-start | bytes 2097152 | tf_op jit(solution)/shard_map/all_to_all | solution.py:31
  126.0 46.8 %all-gather.3.cloned.1.call-start = ((), (), s32[]{:S(2)}) async-start(), calls=%async_computation.7 | async-start | bytes 1114112 | tf_op jit(solution)/shard_map/all_gather | solution.py:210
  128.1 11.1 %collective-permute-start.11 = (bf16[256,512]{1,0:T(8,128)(2,1)S(1)}, bf16[256,512]{1,0:T(8,128)(2,1)S(1)}, u32[]{:S(2)}, u32[]{:S(2)}) collective-permute-start(bf16[256,512]{1,0:T(8,128)(2,1)S(1)} %fusion.2.refs_0_), channel_id=1, source_target_pairs={{0,4},{4,8},{8,12},{12,0},{1,5},{5,9},{9,13},{13,1},{2,6},{6,10},{... | collective-permute-start | bytes 786440 | tf_op jit(solution)/shard_map/ppermute | solution.py:40
  130.0 12.7 %collective-permute-start.12 = (bf16[256,512]{1,0:T(8,128)(2,1)S(1)}, bf16[256,512]{1,0:T(8,128)(2,1)S(1)}, u32[]{:S(2)}, u32[]{:S(2)}) collective-permute-start(bf16[256,512]{1,0:T(8,128)(2,1)S(1)} %fusion.2.refs_0_), channel_id=1, source_target_pairs={{0,8},{4,12},{8,0},{12,4},{1,9},{5,13},{9,1},{13,5},{2,10},{6,14},... | collective-permute-start | bytes 786440 | tf_op jit(solution)/shard_map/ppermute | solution.py:40
  135.4 10.6 %collective-permute-start.13 = (bf16[256,512]{1,0:T(8,128)(2,1)S(1)}, bf16[256,512]{1,0:T(8,128)(2,1)S(1)}, u32[]{:S(2)}, u32[]{:S(2)}) collective-permute-start(bf16[256,512]{1,0:T(8,128)(2,1)S(1)} %fusion.2.refs_0_), channel_id=1, source_target_pairs={{0,12},{4,0},{8,4},{12,8},{1,13},{5,1},{9,5},{13,9},{2,14},{6,2},{... | collective-permute-start | bytes 786440 | tf_op jit(solution)/shard_map/ppermute | solution.py:40
  151.1 29.5 %all-to-all-start.4 = ((f16[4,256,512]{2,1,0:T(8,128)(2,1)}), f16[4,256,512]{2,1,0:T(8,128)(2,1)}, u32[]{:S(2)}, u32[]{:S(2)}) async-start(f16[4,256,512]{2,1,0:T(8,128)(2,1)} %bitcast.31), calls=%async_computation.5 | async-start | bytes 2097152 | tf_op jit(solution)/shard_map/all_to_all | solution.py:31
  172.8 1.2 copy-start.2
Sparse Core Ops, SparseCore 0:
  26.8 39.9 reduce-scatter.1
  129.1 43.5 all-gather.2
